TPU v7x, 32 devices: a whole 2x2x4 slice. The times are simulated.
32 devices in a mesh: freq: 8 (over z, y), sta: 4 (over x, core).
Axes of the slice: x: 2, y: 2, z: 4, core: 2. Of those that a mesh axis runs over, the one named last changes fastest.
Arguments:
- spectra: float32 [2, 128, 64, 8192], P(None, 'freq', None, 'sta'), may hold values from -24 to 24
- current: float32 [64, 2, 128, 512], P('freq', None, None, 'sta'), may hold values from -600 to 600, as said below
- previous: float32 [64, 2, 128, 512], P('freq', None, None, 'sta'), may hold values from -600 to 600, as said below
- table: int32 [64, 512], replicated, may hold values from 0 to 16383
- station_block: int32 [8192], P('sta'), may hold values from 0 to 63
- offsets: float32 [2, 8192], P(None, 'sta'), may hold values from -4 to 4
- slowness: float32 [2, 512], replicated, may hold values from -3 to 3
- weights: float32 [512], P('sta'), may hold values from 400 to 5000
- momentum: float32 [1], replicated, may hold values from 2 to 10
Outputs:
- estimate: float32 [64, 2, 128, 512], P('freq', None, None, 'sta')
- extrapolated: float32 [64, 2, 128, 512], P('freq', None, None, 'sta')
Inputs may be any that keep to these rules, and one draw needn't show every extreme that they name: `current`: real values. `previous`: real values.
All inputs are finite; a program needn't handle non-finite values.
Results may differ from a plain program's by a relative error of at most 0.00105.
The roundings to bfloat16 on the way count: a program that leaves them out, or rounds other values in their place, can miss the bound.
Values may be sent and summed in bfloat16 or wider, within the bound.
A program may use at most 192 MiB of HBM per device.

v0:
```python
import functools
import math

import jax
import jax.numpy as jnp
from jax import lax
from jax.experimental import pallas as pl
from jax.experimental.pallas import tpu as pltpu
from jax.sharding import PartitionSpec as P

F = 64
CELLS = 512


def cell_block(cell_count):
    block_len = cell_count
    while block_len > 512 and block_len % 2 == 0:
        block_len = block_len // 2
    return block_len


def phases(number, delay_rows, off_rows, slow_cols, period):
    wrapped = number * delay_rows % period
    geometry = (
        off_rows[0][:, None] * slow_cols[0][None, :] + off_rows[1][:, None] * slow_cols[1][None, :]
    )
    phase_angle = (wrapped.astype(jnp.float32) + number.astype(jnp.float32) * geometry) * (
        2.0 * math.pi / period
    )
    return (jnp.cos(phase_angle).astype(jnp.bfloat16), jnp.sin(phase_angle).astype(jnp.bfloat16))


def forward_terms(cos_part, sin_part, iterate):
    window_count = iterate.shape[1]
    stacked = iterate.reshape(2 * window_count, iterate.shape[2])
    contract = (((1,), (1,)), ((), ()))
    with_cos = lax.dot_general(stacked, cos_part, contract, preferred_element_type=jnp.float32)
    with_sin = lax.dot_general(stacked, sin_part, contract, preferred_element_type=jnp.float32)
    real_part = with_cos[:window_count] + with_sin[window_count:]
    imag_part = with_cos[window_count:] - with_sin[:window_count]
    return jnp.stack([real_part, imag_part])


def adjoint_terms(cos_part, sin_part, residual):
    window_count = residual.shape[1]
    stacked = residual.reshape(2 * window_count, residual.shape[2])
    with_cos = jnp.dot(stacked, cos_part, preferred_element_type=jnp.float32)
    with_sin = jnp.dot(stacked, sin_part, preferred_element_type=jnp.float32)
    real_part = with_cos[:window_count] - with_sin[window_count:]
    imag_part = with_cos[window_count:] + with_sin[:window_count]
    return jnp.stack([real_part, imag_part])


def local(spectra, current, previous, table, station_block, offsets, slowness, weights, momentum):
    period = 4 * F
    normalizer = 1.0 / math.sqrt(CELLS)
    bin_count = current.shape[0]
    cell_share = current.shape[3]
    stations_here = station_block.shape[0]
    station_total = stations_here * lax.axis_size("sta")
    first_bin = lax.axis_index("freq") * bin_count
    relaid = lax.all_to_all(
        spectra.astype(jnp.bfloat16), "freq", split_axis=2, concat_axis=1, tiled=True
    ).astype(spectra.dtype)
    iterate_b = current.astype(jnp.bfloat16)
    segment = lax.all_gather(iterate_b, "sta", axis=3, tiled=True)
    cell_count = segment.shape[3]
    block_len = cell_block(cell_count)
    delay_rows = jnp.take(table, station_block, axis=0)
    bin_terms = []
    cos_blocks = []
    sin_blocks = []
    for add_bin_index in range(bin_count):
        cos_part, sin_part = phases(
            first_bin + add_bin_index + 1, delay_rows, offsets, slowness, period
        )
        cos_blocks.append(cos_part)
        sin_blocks.append(sin_part)
        bin_terms.append(
            forward_terms(cos_part, sin_part, segment[add_bin_index, :, :, 0:block_len])
        )
    running = jnp.stack(bin_terms)
    cos_all = jnp.stack(cos_blocks)
    sin_all = jnp.stack(sin_blocks)
    predicted, cos_all, sin_all = (running, cos_all, sin_all)
    bin_sums = []
    for bin_index in range(bin_count):
        residual = (predicted[bin_index] * normalizer - relaid[:, :, bin_index, :]).astype(
            jnp.bfloat16
        )
        bin_sums.append(
            adjoint_terms(cos_all[bin_index], sin_all[bin_index], residual) * normalizer
        )
    partial_sums = jnp.stack(bin_sums)
    summed = lax.psum(partial_sums, "sta")
    gradient = lax.dynamic_slice_in_dim(summed, lax.axis_index("sta") * cell_share, cell_share, 3)
    step_size = CELLS / (math.sqrt(station_total) + math.sqrt(CELLS)) ** 2
    stepped = current - step_size * gradient
    threshold = step_size * weights
    squares = jnp.sum(stepped * stepped, axis=(0, 1))
    group_norm = jnp.sqrt(lax.psum(squares, "freq") + 1e-06)
    estimate = stepped * jnp.maximum(0.0, 1.0 - threshold[None, :] / group_norm)
    momentum_now = momentum[0]
    momentum_next = (1.0 + jnp.sqrt(1.0 + 4.0 * momentum_now * momentum_now)) / 2.0
    extrapolated = estimate + (momentum_now - 1.0) / momentum_next * (estimate - previous)
    return (estimate, extrapolated)


SIN_TERMS = (3.1415926535362892, -5.167712764624382, 2.5501633189428987, -0.5992521977810126, 0.08205040162239277, -0.007028386120383206)
COS_TERMS = (0.9999999997799041, -4.934802137078749, 4.058709159554242, -1.335212003029471, 0.23493731372678894, -0.024396324214549327)


def horner(terms, u):
    total = jnp.full_like(u, terms[-1])
    for term in terms[-2::-1]:
        total = total * u + term
    return total


def turns_cos_sin(turns):
    part = turns - jnp.round(turns)
    square = part * part
    half_sin = part * horner(SIN_TERMS, square)
    half_cos = horner(COS_TERMS, square)
    doubled = half_sin + half_sin
    return 1.0 - doubled * half_sin, doubled * half_cos


def angles_kernel(
    period, numbers_ref, blocks_ref, off_ref, tab_ref, slow_ref, uc_ref, us_ref, ac_ref, as_ref, bc_ref, bs_ref, delay_ref
):
    cells, tile = delay_ref.shape
    rows = lax.broadcasted_iota(jnp.int32, (tab_ref.shape[1], tile), 0)
    picks = jnp.where(rows == blocks_ref[...], 1.0, 0.0).astype(jnp.bfloat16)
    delay_ref[...] = jnp.dot(tab_ref[...], picks, preferred_element_type=jnp.float32)
    scale = 1.0 / period
    strip = 16
    lanes = 256

    def fill(index, _):
        row = pl.ds(pl.multiple_of(index // (tile // lanes) * strip, strip), strip)
        col = pl.ds(pl.multiple_of(index % (tile // lanes) * lanes, lanes), lanes)
        slow = slow_ref[row, :]
        geometry = off_ref[0:1, col] * slow[:, 0:1] + off_ref[1:2, col] * slow[:, 1:2]
        delay = delay_ref[row, col]
        uc_ref[row, col], us_ref[row, col] = turns_cos_sin((delay + geometry) * scale)
        for c, (cos_out, sin_out) in enumerate(((ac_ref, as_ref), (bc_ref, bs_ref))):
            number = numbers_ref[c].astype(jnp.float32)
            turns = number * delay * scale
            turns = (turns - jnp.round(turns)) + number * geometry * scale
            cos_out[row, col], sin_out[row, col] = turns_cos_sin(turns)
        return 0

    lax.fori_loop(0, cells // strip * (tile // lanes), fill, 0, unroll=2)


def angles(numbers, blocks, offsets, tab, slow, period):
    cells = tab.shape[0]
    stations = blocks.shape[1]
    tile = 512
    whole = lambda shape: pl.BlockSpec(shape, lambda i: (0,) * len(shape))
    return pl.pallas_call(
        functools.partial(angles_kernel, period),
        grid=(stations // tile,),
        out_shape=[jax.ShapeDtypeStruct((cells, stations), jnp.float32)] * 6,
        in_specs=[
            pl.BlockSpec(memory_space=pltpu.SMEM),
            pl.BlockSpec((1, tile), lambda i: (0, i)),
            pl.BlockSpec((2, tile), lambda i: (0, i)),
            whole(tab.shape),
            whole(slow.shape),
        ],
        out_specs=[pl.BlockSpec((cells, tile), lambda i: (0, i))] * 6,
        scratch_shapes=[pltpu.VMEM((cells, tile), jnp.float32)],
        compiler_params=pltpu.CompilerParams(vmem_limit_bytes=52 * 2**20),
        cost_estimate=pl.CostEstimate(flops=25 * 10**9, bytes_accessed=24 * cells * stations, transcendentals=0),
    )(numbers, blocks, offsets, tab, slow)


def bins_kernel(
    normalizer, place_ref, uc_ref, us_ref, fc_ref, fs_ref, x_ref, o0, o1, o2, o3, g_ref,
    cos_ref, sin_ref, pred_ref, res_ref
):
    bins, cells, tile = cos_ref.shape
    spot = place_ref[0]
    windows = x_ref.shape[1] // 2
    piece = o0.shape[2]
    step = pl.program_id(0)

    @pl.when(step == 0)
    def _():
        g_ref[...] = jnp.zeros_like(g_ref)

    strip = 16
    lanes = 256

    def fill(index, _):
        row = pl.ds(pl.multiple_of(index // (tile // lanes) * strip, strip), strip)
        col = pl.ds(pl.multiple_of(index % (tile // lanes) * lanes, lanes), lanes)
        unit_cos, unit_sin = uc_ref[row, col], us_ref[row, col]
        cos_old, sin_old = fc_ref[row, col], fs_ref[row, col]
        cos_ref[0, row, col] = cos_old.astype(jnp.bfloat16)
        sin_ref[0, row, col] = sin_old.astype(jnp.bfloat16)
        cos_now = cos_old * unit_cos - sin_old * unit_sin
        sin_now = sin_old * unit_cos + cos_old * unit_sin
        twice = unit_cos + unit_cos
        for b in range(1, bins):
            cos_ref[b, row, col] = cos_now.astype(jnp.bfloat16)
            sin_ref[b, row, col] = sin_now.astype(jnp.bfloat16)
            if b < bins - 1:
                cos_now, cos_old = twice * cos_now - cos_old, cos_now
                sin_now, sin_old = twice * sin_now - sin_old, sin_now
        return 0

    lax.fori_loop(0, cells // strip * (tile // lanes), fill, 0, unroll=2)

    across = (((1,), (1,)), ((), ()))

    for b in range(bins):
        stacked = x_ref[b]
        with_cos = jnp.dot(stacked, cos_ref[b], preferred_element_type=jnp.float32)
        with_sin = jnp.dot(stacked, sin_ref[b], preferred_element_type=jnp.float32)
        pred_ref[b, 0:windows] = (with_cos[:windows] + with_sin[windows:]) * normalizer
        pred_ref[b, windows:] = (with_cos[windows:] - with_sin[:windows]) * normalizer
        for d, o_ref in enumerate((o0, o1, o2, o3)):
            first = jnp.bitwise_xor(spot, d) * piece
            for k in range(2):
                at = pl.ds(pl.multiple_of(first + k * windows, piece), piece)
                res_ref[b, at, :] = (pred_ref[b, at, :] - o_ref[b, k].astype(jnp.float32)).astype(jnp.bfloat16)
        residual = res_ref[b]
        back_cos = lax.dot_general(residual, cos_ref[b], across, preferred_element_type=jnp.float32)
        back_sin = lax.dot_general(residual, sin_ref[b], across, preferred_element_type=jnp.float32)
        g_ref[b, 0:windows] += back_cos[:windows] - back_sin[windows:]
        g_ref[b, windows:] += back_cos[windows:] + back_sin[:windows]


def bins_gradient(place, unit, first, iterate, observed, normalizer):
    bins, rows, cells = iterate.shape
    stations = unit[0].shape[1]
    piece = observed[0].shape[2]
    tile = 512
    vm = pltpu.VMEM
    whole = lambda shape: pl.BlockSpec(shape, lambda i: (0,) * len(shape))
    return pl.pallas_call(
        functools.partial(bins_kernel, normalizer),
        grid=(stations // tile,),
        out_shape=jax.ShapeDtypeStruct((bins, rows, cells), jnp.float32),
        in_specs=[
            pl.BlockSpec(memory_space=pltpu.SMEM),
        ]
        + [pl.BlockSpec((cells, tile), lambda i: (0, i))] * 4
        + [whole(iterate.shape)]
        + [pl.BlockSpec((bins, 2, piece, tile), lambda i: (0, 0, 0, i))] * 4,
        out_specs=whole((bins, rows, cells)),
        scratch_shapes=[
            vm((bins, cells, tile), jnp.bfloat16),
            vm((bins, cells, tile), jnp.bfloat16),
            vm((bins, rows, tile), jnp.float32),
            vm((bins, rows, tile), jnp.bfloat16),
        ],
        compiler_params=pltpu.CompilerParams(vmem_limit_bytes=52 * 2**20),
        cost_estimate=pl.CostEstimate(
            flops=8 * bins * rows * cells * stations, bytes_accessed=16 * 2**20, transcendentals=0
        ),
    )(place, *unit, *first, iterate, *observed)


def local_grouped(freq_size, sta_size, spectra, current, previous, table, station_block, offsets, slowness, weights, momentum):
    period = 4 * F
    normalizer = 1.0 / math.sqrt(CELLS)
    bins = current.shape[0]
    cell_share = current.shape[3]
    half_windows = current.shape[2] // 2
    stations_here = station_block.shape[0]
    station_total = stations_here * sta_size
    me = lax.axis_index("freq")
    mine = lax.axis_index("sta")
    half, spot = me // 4, me % 4
    gradient_back = []
    rounded = current.astype(jnp.bfloat16)
    tab = jnp.bitwise_and(table, period - 1).astype(jnp.bfloat16).T
    slow = slowness.T
    blocks = station_block.reshape(1, -1)
    picks = []
    iterates = []
    for c in range(2):
        give = lax.rem(me + c, 2)
        sent = lax.dynamic_slice_in_dim(rounded, give * half_windows, half_windows, 2)
        perm = [(f, ((f + c) % 2) * 4 + f // 2) for f in range(freq_size)]
        got = lax.ppermute(sent, "freq", perm)
        iterates.append(got)
        gradient_back.append([(b, a) for a, b in perm])
    observed = []
    for c in range(2):
        odd = lax.rem(half + c, 2)
        parts = []
        for d in range(4):
            first = (2 * jnp.bitwise_xor(spot, d) + odd) * bins
            part = lax.dynamic_slice_in_dim(spectra, first, bins, 2).astype(jnp.bfloat16)
            parts.append(jnp.transpose(part, (2, 0, 1, 3)))
        if c == 0:
            parts, iterates = lax.optimization_barrier((parts, iterates))
            iterates = lax.all_gather(jnp.stack(iterates), "sta", axis=4, tiled=True)
        for d in range(1, 4):
            parts[d] = lax.ppermute(parts[d], "freq", [(f, f ^ d) for f in range(freq_size)])
        observed.append(parts)
    halves = []
    numbers = jnp.stack([(2 * spot + lax.rem(half + c, 2)) * bins + 1 for c in range(2)]).astype(jnp.int32)
    trig = angles(numbers, blocks, offsets, tab, slow, period)
    place = spot.reshape(1).astype(jnp.int32)
    for c in range(2):
        iterate = iterates[c].reshape(bins, 2 * half_windows, cell_share * sta_size)
        partial = bins_gradient(
            place, trig[0:2], trig[2 * c + 2 : 2 * c + 4], iterate, observed[c], normalizer
        )
        share = lambda d: lax.dynamic_slice_in_dim(
            partial, jnp.bitwise_xor(mine, d) * cell_share, cell_share, 2
        )
        swap = lambda block, d: lax.ppermute(block, "sta", [(s, s ^ d) for s in range(sta_size)])
        across = share(2) + swap(share(3), 1)
        total = share(0) + swap(share(1), 1) + swap(across, 2)
        home = lax.ppermute(total * normalizer, "freq", gradient_back[c])
        halves.append(home.reshape(bins, 2, half_windows, cell_share))
    even = lax.rem(me, 2) == 0
    gradient = jnp.concatenate(
        [jnp.where(even, halves[0], halves[1]), jnp.where(even, halves[1], halves[0])], axis=2
    )
    step_size = CELLS / (math.sqrt(station_total) + math.sqrt(CELLS)) ** 2
    stepped = current - step_size * gradient
    threshold = step_size * weights
    squares = jnp.sum(stepped * stepped, axis=(0, 1))
    for d in (1, 2, 4):
        squares = squares + lax.ppermute(squares, "freq", [(f, f ^ d) for f in range(freq_size)])
    group_norm = jnp.sqrt(squares + 1e-06)
    estimate = stepped * jnp.maximum(0.0, 1.0 - threshold[None, :] / group_norm)
    momentum_now = momentum[0]
    momentum_next = (1.0 + jnp.sqrt(1.0 + 4.0 * momentum_now * momentum_now)) / 2.0
    extrapolated = estimate + (momentum_now - 1.0) / momentum_next * (estimate - previous)
    return (estimate, extrapolated)


def solution(mesh):
    freq_size, sta_size = mesh.shape["freq"], mesh.shape["sta"]
    body = local
    if freq_size == 8 and sta_size == 4:
        body = functools.partial(local_grouped, freq_size, sta_size)
    in_specs = (
        P(None, "freq", None, "sta"),
        P("freq", None, None, "sta"),
        P("freq", None, None, "sta"),
        P(),
        P("sta"),
        P(None, "sta"),
        P(),
        P("sta"),
        P(),
    )
    out_specs = (P("freq", None, None, "sta"), P("freq", None, None, "sta"))
    return jax.shard_map(body, mesh=mesh, in_specs=in_specs, out_specs=out_specs, check_vma=False)
```

profile of v0, /device:TPU:0, one launch (start us, length us, event | category | flops | bytes accessed | tf_op | source)
XLA Modules:
  0.0 236.8 jit_solution(2516016379379864089)
XLA Ops:
  7.2 0.0 all-gather.2.cloned.1.call-start
  7.2 1.3 convert_element_type.35
  8.6 0.7 constant_dynamic-slice_fusion.8
  9.3 3.6 %collective-permute-start = (bf16[8,2,64,128]{3,2,1,0:T(8,128)(2,1)}, bf16[8,2,64,128]{3,2,1,0:T(8,128)(2,1)}, u32[]{:S(2)}, u32[]{:S(2)}) collective-permute-start(bf16[8,2,64,128]{3,2,1,0:T(8,128)(2,1)} %get-tuple-element.45), channel_id=1, source_target_pairs={{0,0},{4,16},{8,4},{12,20},{16,8},{20,24},{24,12},{28,28},{1,1},{5... | collective-permute-start | bytes 786440 | tf_op jit(solution)/shard_map/ppermute | solution.py:290
  12.9 2.8 %collective-permute-start.1 = (bf16[8,2,64,128]{3,2,1,0:T(8,128)(2,1)S(1)}, bf16[8,2,64,128]{3,2,1,0:T(8,128)(2,1)}, u32[]{:S(2)}, u32[]{:S(2)}) collective-permute-start(bf16[8,2,64,128]{3,2,1,0:T(8,128)(2,1)S(1)} %get-tuple-element.44), channel_id=1, source_target_pairs={{0,16},{4,0},{8,20},{12,4},{16,24},{20,8},{24,28},{28,12},{1,17},{... | collective-permute-start | bytes 786440 | tf_op jit(solution)/shard_map/ppermute | solution.py:290
  15.7 8.8 %constant_dynamic-slice_fusion.2 = (bf16[2,16,8,2048]{3,2,1,0:T(8,128)(2,1)S(1)}, bf16[2,16,8,2048]{3,2,1,0:T(8,128)(2,1)}, bf16[2,16,8,2048]{3,2,1,0:T(8,128)(2...) fusion(f32[2,16,64,2048]{3,2,1,0:T(8,128)} %param.9, ...), kind=kLoop, calls=%fused_computation.33 | loop fusion | bytes 16777248 | tf_op jit(solution)/shard_map/dynamic_slice | solution.py:299
  24.6 4.2 %fusion = (bf16[8,2,16,2048]{3,2,1,0:T(8,128)(2,1)}, bf16[8,2,16,2048]{3,2,1,0:T(8,128)(2,1)}) fusion(bf16[2,16,8,2048]{3,2,1,0:T(8,128)(2,1)} %get-tuple-element.35, bf16[2,16,8,2048]{3,2,1,0:T(8,128)(2,1)} %get-tuple-element.34), kind=kLoop, calls=%fused_computation.8 | loop fusion | bytes 4194304 | tf_op jit(solution)/shard_map/transpose | solution.py:300
  28.8 2.5 %fusion.2 = (bf16[8,2,16,2048]{3,2,1,0:T(8,128)(2,1)}, bf16[8,2,16,2048]{3,2,1,0:T(8,128)(2,1)}) fusion(bf16[2,16,8,2048]{3,2,1,0:T(8,128)(2,1)S(1)} %copy-done.4, bf16[2,16,8,2048]{3,2,1,0:T(8,128)(2,1)S(1)} %copy-done.3), kind=kLoop, calls=%fused_computation.10 | loop fusion | bytes 4194304 | tf_op jit(solution)/shard_map/transpose | solution.py:300
  31.3 0.0 collective-permute-done
  31.3 0.0 collective-permute-done.1
  31.3 1.9 pad_maximum_fusion
  33.2 0.0 all-gather.2.cloned.1.call-update
  33.2 2.8 %copy.66 = bf16[2,16,8,2048]{3,1,0,2:T(8,128)(2,1)} copy(bf16[2,16,8,2048]{3,2,1,0:T(8,128)(2,1)} %get-tuple-element.29) | data formatting | bytes 2097152
  36.0 2.6 %collective-permute-start.10 = (bf16[8,2,16,2048]{3,2,1,0:T(8,128)(2,1)}, bf16[8,2,16,2048]{3,2,1,0:T(8,128)(2,1)}, u32[]{:S(2)}, u32[]{:S(2)}) collective-permute-start(bf16[8,2,16,2048]{3,2,1,0:T(8,128)(2,1)} %bitcast.32), channel_id=1, source_target_pairs={{0,8},{4,12},{8,0},{12,4},{16,24},{20,28},{24,16},{28,20},{1,9},{5... | collective-permute-start | bytes 3145736 | tf_op jit(solution)/shard_map/ppermute | solution.py:305
  38.6 1.5 copy.67
  40.1 0.0 collective-permute-start.11
  40.1 0.6 copy.65
  40.7 1.5 collective-permute-start.9
  42.2 0.1 copy.21
  42.4 0.1 copy.23
  42.5 0.1 pad_add_fusion.numbers_ref
  42.7 28.4 %shard_map.104 = (f32[512,2048]{1,0:T(8,128)}, f32[512,2048]{1,0:T(8,128)}, f32[512,2048]{1,0:T(8,128)}, f32[512,2048]{1,0:T(8,128)}, f32[512,2048]{1,0:T(8,128)}, /*index=5*/f32[512,2048]{1,0:T(8,128)}) custom-call(s32[2]{0:T(128)S(1)} %pad_add_fusion.numbers_ref, s32[1,2048]{1,0:T(1,128)S(1)} %bitcast.40, f32[2,2048]{1,0:T(2,128)S(1)} %copy-done, ...), custom_call_target="tpu_custom_call" | custom-call | flops 24999999488 | bytes 25165824 | tf_op jit(solution)/shard_map/pallas_call | solution.py:162
  71.0 1.5 copy.64
  72.6 0.6 collective-permute-start.2
  73.2 1.9 collective-permute-start.3
  75.0 0.0 collective-permute-done.10.o2
  75.1 1.1 collective-permute-start.4
  76.1 1.7 fusion.10
  77.9 7.6 %collective-permute-done.11.o3 = bf16[8,2,16,2048]{3,2,1,0:T(8,128)(2,1)} collective-permute-done((bf16[8,2,16,2048]{3,2,1,0:T(8,128)(2,1)}, bf16[8,2,16,2048]{3,2,1,0:T(8,128)(2,1)}, u32[]{:S(2)}, u32[]{:S(2)}) %collective-permute-start.11) | collective-permute-done | bytes 1048608 | tf_op jit(solution)/shard_map/ppermute | solution.py:305
  85.5 4.0 %collective-permute-done.9.o1 = bf16[8,2,16,2048]{3,2,1,0:T(8,128)(2,1)} collective-permute-done((bf16[8,2,16,2048]{3,2,1,0:T(8,128)(2,1)S(1)}, bf16[8,2,16,2048]{3,2,1,0:T(8,128)(2,1)}, u32[]{:S(2)}, u32[]{:S(2)}) %collective-permute-start.9) | collective-permute-done | bytes 1048608 | tf_op jit(solution)/shard_map/ppermute | solution.py:305
  89.5 31.6 %shard_map.106 = f32[8,128,512]{2,1,0:T(8,128)} custom-call(s32[1]{0:T(128)} %bitcast.place_ref, f32[512,2048]{1,0:T(8,128)} %get-tuple-element.14.uc_ref, f32[512,2048]{1,0:T(8,128)} %get-tuple-element.15.us_ref, f32[512,2048]{1,0:T(8,128)} %get-tuple-element.24.fc_ref, f32[512,2048]{1,0:T(8,128)} %get-tuple-element.25.fs_ref, ...), custom_call_target="tpu_custom_call" | custom-call | flops 8589934592 | bytes 16777216 | tf_op jit(solution)/shard_map/pallas_call | solution.py:244
  121.0 2.3 constant_dynamic-slice_fusion.1
  123.3 0.0 collective-permute-start.13
  123.4 8.9 %collective-permute-done.2.o1 = bf16[8,2,16,2048]{3,2,1,0:T(8,128)(2,1)S(1)} collective-permute-done((bf16[8,2,16,2048]{3,2,1,0:T(8,128)(2,1)}, bf16[8,2,16,2048]{3,2,1,0:T(8,128)(2,1)S(1)}, u32[]{:S(2)}, u32[]{:S(2)}) %collective-permute-start.2) | collective-permute-done | bytes 1048608 | tf_op jit(solution)/shard_map/ppermute | solution.py:305
  132.3 0.0 collective-permute-done.4.o3
  132.3 1.0 copy-done.11
  133.2 31.6 %shard_map.105 = f32[8,128,512]{2,1,0:T(8,128)} custom-call(s32[1]{0:T(128)} %bitcast.place_ref, f32[512,2048]{1,0:T(8,128)} %get-tuple-element.14.uc_ref, f32[512,2048]{1,0:T(8,128)} %get-tuple-element.15.us_ref, f32[512,2048]{1,0:T(8,128)} %get-tuple-element.16.fc_ref, f32[512,2048]{1,0:T(8,128)} %get-tuple-element.17.fs_ref, ...), custom_call_target="tpu_custom_call" | custom-call | flops 8589934592 | bytes 16777216 | tf_op jit(solution)/shard_map/pallas_call | solution.py:244
  164.8 2.4 %constant_dynamic-slice_fusion.7 = (f32[8,128,128]{2,1,0:T(8,128)}, f32[8,128,128]{2,1,0:T(8,128)}) fusion(f32[8,128,512]{2,1,0:T(8,128)} %shard_map.105, s32[]{:T(128)S(6)} %select_n.85, s32[]{:T(128)S(6)} %select_n.87), kind=kLoop, calls=%fused_computation.38 | loop fusion | bytes 2097160 | tf_op jit(solution)/shard_map/dynamic_slice | solution.py:316
  167.2 0.0 collective-permute-start.6
  167.2 0.5 collective-permute-start.12
  167.8 0.9 dynamic-slice_add_fusion
  168.7 1.5 collective-permute-start.14
  170.1 0.1 collective-permute-done.6
  170.2 2.0 dynamic-slice_add_fusion.1
  172.3 1.5 collective-permute-start.7
  173.7 0.0 collective-permute-done.12
  173.7 10.0 %collective-permute-done.14 = f32[8,128,128]{2,1,0:T(8,128)} collective-permute-done((f32[8,128,128]{2,1,0:T(8,128)}, f32[8,128,128]{2,1,0:T(8,128)}, u32[]{:S(2)}, u32[]{:S(2)}) %collective-permute-start.14) | collective-permute-done | bytes 524320 | tf_op jit(solution)/shard_map/ppermute | solution.py:319
  183.8 1.9 add_multiply_fusion
  185.7 1.5 collective-permute-start.15
  187.2 0.0 collective-permute-done.5
  187.2 6.9 %collective-permute-done.7 = f32[8,128,128]{2,1,0:T(8,128)} collective-permute-done((f32[8,128,128]{2,1,0:T(8,128)}, f32[8,128,128]{2,1,0:T(8,128)}, u32[]{:S(2)}, u32[]{:S(2)}) %collective-permute-start.7) | collective-permute-done | bytes 524320 | tf_op jit(solution)/shard_map/ppermute | solution.py:319
  194.0 1.3 add_multiply_fusion.1
  195.3 1.4 collective-permute-start.8
  196.8 2.1 collective-permute-done.15
  198.9 0.8 copy-done.8
  199.7 1.3 broadcast_select_fusion.1
  201.0 0.1 multiply_reduce_fusion
  201.1 14.0 %collective-permute-start.16 = (f32[128,128]{1,0:T(8,128)S(1)}, f32[128,128]{1,0:T(8,128)S(1)}, u32[]{:S(2)}, u32[]{:S(2)}) collective-permute-start(f32[128,128]{1,0:T(8,128)S(1)} %multiply_reduce_fusion), channel_id=1, source_target_pairs={{0,4},{4,0},{8,12},{12,8},{16,20},{20,16},{24,28},{28,24},{1,5},{5... | collective-permute-start | bytes 196616 | tf_op jit(solution)/shard_map/ppermute | solution.py:333
  215.1 2.2 collective-permute-done.16
  217.4 1.4 collective-permute-start.17
  218.7 3.6 %collective-permute-done.17 = f32[128,128]{1,0:T(8,128)S(1)} collective-permute-done((f32[128,128]{1,0:T(8,128)S(1)}, f32[128,128]{1,0:T(8,128)S(1)}, u32[]{:S(2)}, u32[]{:S(2)}) %collective-permute-start.17) | collective-permute-done | bytes 65568 | tf_op jit(solution)/shard_map/ppermute | solution.py:333
  222.3 1.7 collective-permute-start.18
  224.8 3.5 %collective-permute-done.18 = f32[128,128]{1,0:T(8,128)S(1)} collective-permute-done((f32[128,128]{1,0:T(8,128)S(1)}, f32[128,128]{1,0:T(8,128)S(1)}, u32[]{:S(2)}, u32[]{:S(2)}) %collective-permute-start.18) | collective-permute-done | bytes 65568 | tf_op jit(solution)/shard_map/ppermute | solution.py:333
  228.3 1.6 multiply_add_fusion
  (34 shorter events, 0.1 us)
Async XLA Ops:
  7.2 69.0 %all-gather.2.cloned.1.call-start = ((), (), s32[]{:S(2)}) async-start(), calls=%async_computation | async-start | bytes 2621440 | tf_op jit(solution)/shard_map/all_gather | solution.py:303
  9.3 22.0 %collective-permute-start = (bf16[8,2,64,128]{3,2,1,0:T(8,128)(2,1)}, bf16[8,2,64,128]{3,2,1,0:T(8,128)(2,1)}, u32[]{:S(2)}, u32[]{:S(2)}) collective-permute-start(bf16[8,2,64,128]{3,2,1,0:T(8,128)(2,1)} %get-tuple-element.45), channel_id=1, source_target_pairs={{0,0},{4,16},{8,4},{12,20},{16,8},{20,24},{24,12},{28,28},{1,1},{5... | collective-permute-start | bytes 786440 | tf_op jit(solution)/shard_map/ppermute | solution.py:290
  12.9 18.4 %collective-permute-start.1 = (bf16[8,2,64,128]{3,2,1,0:T(8,128)(2,1)S(1)}, bf16[8,2,64,128]{3,2,1,0:T(8,128)(2,1)}, u32[]{:S(2)}, u32[]{:S(2)}) collective-permute-start(bf16[8,2,64,128]{3,2,1,0:T(8,128)(2,1)S(1)} %get-tuple-element.44), channel_id=1, source_target_pairs={{0,16},{4,0},{8,20},{12,4},{16,24},{20,8},{24,28},{28,12},{1,17},{... | collective-permute-start | bytes 786440 | tf_op jit(solution)/shard_map/ppermute | solution.py:290
  24.6 4.2 %copy-start.3 = (bf16[2,16,8,2048]{3,2,1,0:T(8,128)(2,1)S(1)}, bf16[2,16,8,2048]{3,2,1,0:T(8,128)(2,1)}, u32[]{:S(2)}) copy-start(bf16[2,16,8,2048]{3,2,1,0:T(8,128)(2,1)} %get-tuple-element.32) | copy-start | bytes 3145732
  24.6 4.2 %copy-start.4 = (bf16[2,16,8,2048]{3,2,1,0:T(8,128)(2,1)S(1)}, bf16[2,16,8,2048]{3,2,1,0:T(8,128)(2,1)}, u32[]{:S(2)}) copy-start(bf16[2,16,8,2048]{3,2,1,0:T(8,128)(2,1)} %get-tuple-element.33) | copy-start | bytes 3145732
  36.0 39.1 %collective-permute-start.10 = (bf16[8,2,16,2048]{3,2,1,0:T(8,128)(2,1)}, bf16[8,2,16,2048]{3,2,1,0:T(8,128)(2,1)}, u32[]{:S(2)}, u32[]{:S(2)}) collective-permute-start(bf16[8,2,16,2048]{3,2,1,0:T(8,128)(2,1)} %bitcast.32), channel_id=1, source_target_pairs={{0,8},{4,12},{8,0},{12,4},{16,24},{20,28},{24,16},{28,20},{1,9},{5... | collective-permute-start | bytes 3145736 | tf_op jit(solution)/shard_map/ppermute | solution.py:305
  38.6 3.7 %copy-start.9 = (s32[64,512]{1,0:T(8,128)S(1)}, s32[64,512]{1,0:T(8,128)}, u32[]{:S(2)}) copy-start(s32[64,512]{1,0:T(8,128)} %param.12) | copy-start | bytes 393220
  38.6 3.8 %copy-start.10 = (f32[2,512]{1,0:T(2,128)S(1)}, f32[2,512]{1,0:T(2,128)}, u32[]{:S(2)}) copy-start(f32[2,512]{1,0:T(2,128)} %param.15) | copy-start | bytes 12292
  40.1 2.5 %copy-start = (f32[2,2048]{1,0:T(2,128)S(1)}, f32[2,2048]{1,0:T(2,128)}, u32[]{:S(2)}) copy-start(f32[2,2048]{1,0:T(2,128)} %off_ref.1) | copy-start | bytes 49156
  40.1 2.5 %copy-start.1 = (s32[2048]{0:T(1024)S(1)}, s32[2048]{0:T(1024)}, u32[]{:S(2)}) copy-start(s32[2048]{0:T(1024)} %param.13) | copy-start | bytes 24580
  40.1 45.3 %collective-permute-start.11 = (bf16[8,2,16,2048]{3,2,1,0:T(8,128)(2,1)}, bf16[8,2,16,2048]{3,2,1,0:T(8,128)(2,1)}, u32[]{:S(2)}, u32[]{:S(2)}) collective-permute-start(bf16[8,2,16,2048]{3,2,1,0:T(8,128)(2,1)} %bitcast.33), channel_id=1, source_target_pairs={{0,12},{4,8},{8,4},{12,0},{16,28},{20,24},{24,20},{28,16},{1,13},{... | collective-permute-start | bytes 3145736 | tf_op jit(solution)/shard_map/ppermute | solution.py:305
  40.7 48.7 %collective-permute-start.9 = (bf16[8,2,16,2048]{3,2,1,0:T(8,128)(2,1)S(1)}, bf16[8,2,16,2048]{3,2,1,0:T(8,128)(2,1)}, u32[]{:S(2)}, u32[]{:S(2)}) collective-permute-start(bf16[8,2,16,2048]{3,2,1,0:T(8,128)(2,1)S(1)} %bitcast.45), channel_id=1, source_target_pairs={{0,4},{4,0},{8,12},{12,8},{16,20},{20,16},{24,28},{28,24},{1,5},{5... | collective-permute-start | bytes 3145736 | tf_op jit(solution)/shard_map/ppermute | solution.py:305
  71.0 4.0 %copy-start.7 = (bf16[8,2,16,2048]{3,2,1,0:T(8,128)(2,1)S(1)}, bf16[8,2,16,2048]{3,2,1,0:T(8,128)(2,1)}, u32[]{:S(2)}) copy-start(bf16[8,2,16,2048]{3,2,1,0:T(8,128)(2,1)} %get-tuple-element.23) | copy-start | bytes 3145732
  72.6 59.7 %collective-permute-start.2 = (bf16[8,2,16,2048]{3,2,1,0:T(8,128)(2,1)}, bf16[8,2,16,2048]{3,2,1,0:T(8,128)(2,1)S(1)}, u32[]{:S(2)}, u32[]{:S(2)}) collective-permute-start(bf16[8,2,16,2048]{3,2,1,0:T(8,128)(2,1)} %get-tuple-element.21), channel_id=1, source_target_pairs={{0,4},{4,0},{8,12},{12,8},{16,20},{20,16},{24,28},{28,24},{1,5},{5... | collective-permute-start | bytes 3145736 | tf_op jit(solution)/shard_map/ppermute | solution.py:305
  73.2 59.1 %collective-permute-start.3 = (bf16[8,2,16,2048]{3,2,1,0:T(8,128)(2,1)}, bf16[8,2,16,2048]{3,2,1,0:T(8,128)(2,1)}, u32[]{:S(2)}, u32[]{:S(2)}) collective-permute-start(bf16[8,2,16,2048]{3,2,1,0:T(8,128)(2,1)} %get-tuple-element.22), channel_id=1, source_target_pairs={{0,8},{4,12},{8,0},{12,4},{16,24},{20,28},{24,16},{28,20},{1,9},{5... | collective-permute-start | bytes 3145736 | tf_op jit(solution)/shard_map/ppermute | solution.py:305
  75.1 57.2 %collective-permute-start.4 = (bf16[8,2,16,2048]{3,2,1,0:T(8,128)(2,1)S(1)}, bf16[8,2,16,2048]{3,2,1,0:T(8,128)(2,1)}, u32[]{:S(2)}, u32[]{:S(2)}) collective-permute-start(bf16[8,2,16,2048]{3,2,1,0:T(8,128)(2,1)S(1)} %copy-done.7), channel_id=1, source_target_pairs={{0,12},{4,8},{8,4},{12,0},{16,28},{20,24},{24,20},{28,16},{1,13},{... | collective-permute-start | bytes 3145736 | tf_op jit(solution)/shard_map/ppermute | solution.py:305
  123.3 44.4 %collective-permute-start.13 = (f32[8,128,128]{2,1,0:T(8,128)}, f32[8,128,128]{2,1,0:T(8,128)S(1)}, u32[]{:S(2)}, u32[]{:S(2)}) collective-permute-start(f32[8,128,128]{2,1,0:T(8,128)} %get-tuple-element.41), channel_id=1, source_target_pairs={{0,1},{1,0},{2,3},{3,2},{4,5},{5,4},{6,7},{7,6},{8,9},{9,8},{10,11... | collective-permute-start | bytes 1572872 | tf_op jit(solution)/shard_map/ppermute | solution.py:319
  132.3 1.0 copy-start.11
  164.8 2.9 %copy-start.5 = (f32[8,128,512]{2,1,0:T(8,128)S(1)}, f32[8,128,512]{2,1,0:T(8,128)}, u32[]{:S(2)}) copy-start(f32[8,128,512]{2,1,0:T(8,128)} %shard_map.106) | copy-start | bytes 6291460
  167.2 3.0 %collective-permute-start.6 = (f32[8,128,128]{2,1,0:T(8,128)}, f32[8,128,128]{2,1,0:T(8,128)}, u32[]{:S(2)}, u32[]{:S(2)}) collective-permute-start(f32[8,128,128]{2,1,0:T(8,128)} %get-tuple-element.37), channel_id=1, source_target_pairs={{0,1},{1,0},{2,3},{3,2},{4,5},{5,4},{6,7},{7,6},{8,9},{9,8},{10,11... | collective-permute-start | bytes 1572872 | tf_op jit(solution)/shard_map/ppermute | solution.py:319
  167.2 6.5 %collective-permute-start.12 = (f32[8,128,128]{2,1,0:T(8,128)}, f32[8,128,128]{2,1,0:T(8,128)S(1)}, u32[]{:S(2)}, u32[]{:S(2)}) collective-permute-start(f32[8,128,128]{2,1,0:T(8,128)} %get-tuple-element.40), channel_id=1, source_target_pairs={{0,1},{1,0},{2,3},{3,2},{4,5},{5,4},{6,7},{7,6},{8,9},{9,8},{10,11... | collective-permute-start | bytes 1572872 | tf_op jit(solution)/shard_map/ppermute | solution.py:319
  168.7 15.1 %collective-permute-start.14 = (f32[8,128,128]{2,1,0:T(8,128)}, f32[8,128,128]{2,1,0:T(8,128)}, u32[]{:S(2)}, u32[]{:S(2)}) collective-permute-start(f32[8,128,128]{2,1,0:T(8,128)} %dynamic-slice_add_fusion), channel_id=1, source_target_pairs={{0,2},{1,3},{2,0},{3,1},{4,6},{5,7},{6,4},{7,5},{8,10},{9,11},{10,... | collective-permute-start | bytes 1572872 | tf_op jit(solution)/shard_map/ppermute | solution.py:319
  170.1 17.0 %collective-permute-start.5 = (f32[8,128,128]{2,1,0:T(8,128)}, f32[8,128,128]{2,1,0:T(8,128)S(1)}, u32[]{:S(2)}, u32[]{:S(2)}) collective-permute-start(f32[8,128,128]{2,1,0:T(8,128)} %get-tuple-element.36), channel_id=1, source_target_pairs={{0,1},{1,0},{2,3},{3,2},{4,5},{5,4},{6,7},{7,6},{8,9},{9,8},{10,11... | collective-permute-start | bytes 1572872 | tf_op jit(solution)/shard_map/ppermute | solution.py:319
  172.3 21.8 %collective-permute-start.7 = (f32[8,128,128]{2,1,0:T(8,128)}, f32[8,128,128]{2,1,0:T(8,128)}, u32[]{:S(2)}, u32[]{:S(2)}) collective-permute-start(f32[8,128,128]{2,1,0:T(8,128)} %dynamic-slice_add_fusion.1), channel_id=1, source_target_pairs={{0,2},{1,3},{2,0},{3,1},{4,6},{5,7},{6,4},{7,5},{8,10},{9,11},{10,... | collective-permute-start | bytes 1572872 | tf_op jit(solution)/shard_map/ppermute | solution.py:319
  185.7 15.3 %copy-start.2 = (f32[8,2,128,128]{3,2,1,0:T(8,128)S(1)}, f32[8,2,128,128]{3,2,1,0:T(8,128)}, u32[]{:S(2)}) copy-start(f32[8,2,128,128]{3,2,1,0:T(8,128)} %param.10) | copy-start | bytes 3145732
  185.7 13.2 %collective-permute-start.15 = (f32[8,128,128]{2,1,0:T(8,128)}, f32[8,128,128]{2,1,0:T(8,128)S(1)}, u32[]{:S(2)}, u32[]{:S(2)}) collective-permute-start(f32[8,128,128]{2,1,0:T(8,128)} %add_multiply_fusion), channel_id=1, source_target_pairs={{16,0},{0,4},{20,8},{4,12},{24,16},{8,20},{28,24},{12,28},{17,1},{... | collective-permute-start | bytes 1572872 | tf_op jit(solution)/shard_map/ppermute | solution.py:322
  195.3 4.3 %collective-permute-start.8 = (f32[8,128,128]{2,1,0:T(8,128)S(1)}, f32[8,128,128]{2,1,0:T(8,128)}, u32[]{:S(2)}, u32[]{:S(2)}) collective-permute-start(f32[8,128,128]{2,1,0:T(8,128)S(1)} %add_multiply_fusion.1), channel_id=1, source_target_pairs={{0,0},{16,4},{4,8},{20,12},{8,16},{24,20},{12,24},{28,28},{1,1},{1... | collective-permute-start | bytes 1572872 | tf_op jit(solution)/shard_map/ppermute | solution.py:322
  196.8 27.3 %copy-start.12 = (f32[128]{0:T(128)S(1)}, f32[128]{0:T(128)}, u32[]{:S(2)}) copy-start(f32[128]{0:T(128)} %param.16) | copy-start | bytes 1540
  196.8 31.5 %copy-start.6 = (f32[8,2,128,128]{3,2,1,0:T(8,128)S(1)}, f32[8,2,128,128]{3,2,1,0:T(8,128)}, u32[]{:S(2)}) copy-start(f32[8,2,128,128]{3,2,1,0:T(8,128)} %param.11) | copy-start | bytes 3145732
  198.9 0.8 copy-start.8
  201.1 16.2 %collective-permute-start.16 = (f32[128,128]{1,0:T(8,128)S(1)}, f32[128,128]{1,0:T(8,128)S(1)}, u32[]{:S(2)}, u32[]{:S(2)}) collective-permute-start(f32[128,128]{1,0:T(8,128)S(1)} %multiply_reduce_fusion), channel_id=1, source_target_pairs={{0,4},{4,0},{8,12},{12,8},{16,20},{20,16},{24,28},{28,24},{1,5},{5... | collective-permute-start | bytes 196616 | tf_op jit(solution)/shard_map/ppermute | solution.py:333
  217.4 5.0 %collective-permute-start.17 = (f32[128,128]{1,0:T(8,128)S(1)}, f32[128,128]{1,0:T(8,128)S(1)}, u32[]{:S(2)}, u32[]{:S(2)}) collective-permute-start(f32[128,128]{1,0:T(8,128)S(1)} %add.166), channel_id=1, source_target_pairs={{0,8},{4,12},{8,0},{12,4},{16,24},{20,28},{24,16},{28,20},{1,9},{5... | collective-permute-start | bytes 196616 | tf_op jit(solution)/shard_map/ppermute | solution.py:333
  222.3 5.9 %collective-permute-start.18 = (f32[128,128]{1,0:T(8,128)S(1)}, f32[128,128]{1,0:T(8,128)S(1)}, u32[]{:S(2)}, u32[]{:S(2)}) collective-permute-start(f32[128,128]{1,0:T(8,128)S(1)} %add.167), channel_id=1, source_target_pairs={{0,16},{4,20},{8,24},{12,28},{16,0},{20,4},{24,8},{28,12},{1,17},{... | collective-permute-start | bytes 196616 | tf_op jit(solution)/shard_map/ppermute | solution.py:333
Sparse Core Ops, SparseCore 0:
  33.3 23.2 all-gather.1
where the time goes:
time: 237 us
  Pallas kernels  91.5 us (39%)
  waiting for transfers between devices  48.9 us (21%)
  starting transfers between devices  37.6 us (16%)
  local copies, waits for them, and re-layouts  31.3 us (13%)
  between operations  14.9 us (6%)
  other arithmetic  12.6 us (5%)
    pallas_call x2, Pallas kernels, bins_gradient(): pl.pallas_call(functools.partial(bins_kernel, normalizer), grid=(stations...  63.2 us
    pallas_call x1, Pallas kernels, angles(): pl.pallas_call(functools.partial(angles_kernel, period), grid=(stations /...  28.4 us
    ppermute x6, waiting for transfers between devices, local_grouped(): lax.ppermute(parts[d], 'freq', [(f, f ^ d) for f in range(freq_size)])  20.5 us
    ppermute x3, starting transfers between devices, local_grouped(): lax.ppermute(squares, 'freq', [(f, f ^ d) for f in range(freq_size)])  17.1 us
    ppermute x6, waiting for transfers between devices, local_grouped(): lax.ppermute(block, 'sta', [(s, s ^ d) for s in range(sta_size)])  17 us
    ppermute x3, waiting for transfers between devices, local_grouped(): lax.ppermute(squares, 'freq', [(f, f ^ d) for f in range(freq_size)])  9.3 us
    dynamic_slice x1, local copies, waits for them, and re-layouts, local_grouped(): lax.dynamic_slice_in_dim(spectra, first, bins, 2).astype(jnp.bfloat16)  8.82 us
    unnamed x32, local copies, waits for them, and re-layouts  8.51 us
  transfers between devices with their start and end apart: 20, of which 10 were waited for; matrix products, arithmetic and copies ran while one was open for 15% of the time, Pallas kernels for 39%

commit v1 on v0

v1 whole, which is shorter than its diff:
```python
import functools
import math

import jax
import jax.numpy as jnp
from jax import lax
from jax.experimental import pallas as pl
from jax.experimental.pallas import tpu as pltpu
from jax.sharding import PartitionSpec as P

F = 64
CELLS = 512


def cell_block(cell_count):
    block_len = cell_count
    while block_len > 512 and block_len % 2 == 0:
        block_len = block_len // 2
    return block_len


def phases(number, delay_rows, off_rows, slow_cols, period):
    wrapped = number * delay_rows % period
    geometry = (
        off_rows[0][:, None] * slow_cols[0][None, :] + off_rows[1][:, None] * slow_cols[1][None, :]
    )
    phase_angle = (wrapped.astype(jnp.float32) + number.astype(jnp.float32) * geometry) * (
        2.0 * math.pi / period
    )
    return (jnp.cos(phase_angle).astype(jnp.bfloat16), jnp.sin(phase_angle).astype(jnp.bfloat16))


def forward_terms(cos_part, sin_part, iterate):
    window_count = iterate.shape[1]
    stacked = iterate.reshape(2 * window_count, iterate.shape[2])
    contract = (((1,), (1,)), ((), ()))
    with_cos = lax.dot_general(stacked, cos_part, contract, preferred_element_type=jnp.float32)
    with_sin = lax.dot_general(stacked, sin_part, contract, preferred_element_type=jnp.float32)
    real_part = with_cos[:window_count] + with_sin[window_count:]
    imag_part = with_cos[window_count:] - with_sin[:window_count]
    return jnp.stack([real_part, imag_part])


def adjoint_terms(cos_part, sin_part, residual):
    window_count = residual.shape[1]
    stacked = residual.reshape(2 * window_count, residual.shape[2])
    with_cos = jnp.dot(stacked, cos_part, preferred_element_type=jnp.float32)
    with_sin = jnp.dot(stacked, sin_part, preferred_element_type=jnp.float32)
    real_part = with_cos[:window_count] - with_sin[window_count:]
    imag_part = with_cos[window_count:] + with_sin[:window_count]
    return jnp.stack([real_part, imag_part])


def local(spectra, current, previous, table, station_block, offsets, slowness, weights, momentum):
    period = 4 * F
    normalizer = 1.0 / math.sqrt(CELLS)
    bin_count = current.shape[0]
    cell_share = current.shape[3]
    stations_here = station_block.shape[0]
    station_total = stations_here * lax.axis_size("sta")
    first_bin = lax.axis_index("freq") * bin_count
    relaid = lax.all_to_all(
        spectra.astype(jnp.bfloat16), "freq", split_axis=2, concat_axis=1, tiled=True
    ).astype(spectra.dtype)
    iterate_b = current.astype(jnp.bfloat16)
    segment = lax.all_gather(iterate_b, "sta", axis=3, tiled=True)
    cell_count = segment.shape[3]
    block_len = cell_block(cell_count)
    delay_rows = jnp.take(table, station_block, axis=0)
    bin_terms = []
    cos_blocks = []
    sin_blocks = []
    for add_bin_index in range(bin_count):
        cos_part, sin_part = phases(
            first_bin + add_bin_index + 1, delay_rows, offsets, slowness, period
        )
        cos_blocks.append(cos_part)
        sin_blocks.append(sin_part)
        bin_terms.append(
            forward_terms(cos_part, sin_part, segment[add_bin_index, :, :, 0:block_len])
        )
    running = jnp.stack(bin_terms)
    cos_all = jnp.stack(cos_blocks)
    sin_all = jnp.stack(sin_blocks)
    predicted, cos_all, sin_all = (running, cos_all, sin_all)
    bin_sums = []
    for bin_index in range(bin_count):
        residual = (predicted[bin_index] * normalizer - relaid[:, :, bin_index, :]).astype(
            jnp.bfloat16
        )
        bin_sums.append(
            adjoint_terms(cos_all[bin_index], sin_all[bin_index], residual) * normalizer
        )
    partial_sums = jnp.stack(bin_sums)
    summed = lax.psum(partial_sums, "sta")
    gradient = lax.dynamic_slice_in_dim(summed, lax.axis_index("sta") * cell_share, cell_share, 3)
    step_size = CELLS / (math.sqrt(station_total) + math.sqrt(CELLS)) ** 2
    stepped = current - step_size * gradient
    threshold = step_size * weights
    squares = jnp.sum(stepped * stepped, axis=(0, 1))
    group_norm = jnp.sqrt(lax.psum(squares, "freq") + 1e-06)
    estimate = stepped * jnp.maximum(0.0, 1.0 - threshold[None, :] / group_norm)
    momentum_now = momentum[0]
    momentum_next = (1.0 + jnp.sqrt(1.0 + 4.0 * momentum_now * momentum_now)) / 2.0
    extrapolated = estimate + (momentum_now - 1.0) / momentum_next * (estimate - previous)
    return (estimate, extrapolated)


SIN_TERMS = (3.1415926535362892, -5.167712764624382, 2.5501633189428987, -0.5992521977810126, 0.08205040162239277, -0.007028386120383206)
COS_TERMS = (0.9999999997799041, -4.934802137078749, 4.058709159554242, -1.335212003029471, 0.23493731372678894, -0.024396324214549327)
MESH = pl.DeviceIdType.MESH
TILE = 512
ROWS = 32
COLS = 256
UNITS = 16
SBUF = 4
STAGE = 2


def horner(terms, u):
    total = jnp.full_like(u, terms[-1])
    for term in terms[-2::-1]:
        total = total * u + term
    return total


def turns_cos_sin(turns):
    part = turns - jnp.round(turns)
    square = part * part
    half_sin = part * horner(SIN_TERMS, square)
    half_cos = horner(COS_TERMS, square)
    doubled = half_sin + half_sin
    return 1.0 - doubled * half_sin, doubled * half_cos


def times(a, b):
    return a[0] * b[0] - a[1] * b[1], a[1] * b[0] + a[0] * b[1]


def twice(a):
    doubled = a[1] + a[1]
    return 1.0 - doubled * a[1], doubled * a[0]


def iteration_kernel(
    period, normalizer, step_size,
    spectra, current, table, blocks, offsets, slowness, weights,
    stepped_out, shrink_out,
    cs_a, cs_b, prev_cos, prev_sin, now_cos, now_sin, unit_cos, unit_sin, chain,
    tab_t, slow_t, delay,
    current_b, x_all, spec_rx, sbuf, stage, own, home, gbuf, rx1, rx2, tx2, keep2, tx3, sums, shrinks,
    x_send, x_recv, y_send, y_recv, s_send, s_recv, l_stage, l_own,
    g1_send, g1_recv, g2_send, g2_recv, g3_send, g3_recv, n_send, n_recv, m_send, m_recv,
):
    me = lax.axis_index("freq")
    sta = lax.axis_index("sta")
    z, y = me // 2, me % 2
    zl, zp = z % 2, z // 2
    x, core = sta // 2, sta % 2
    tiles = cs_a.shape[1]

    def pick(ph, first, second):
        return jnp.where(ph == 0, first, second)

    def block_of(ph, fd, m):
        return pick(ph, fd // 2 * 2 + m, (fd // 4 * 2 + m) * 2 + fd % 2)

    def residue_of(ph, fd):
        return pick(ph, 2 * (fd % 2), 1 + 2 * (fd // 2 % 2))

    def member(ph):
        return pick(ph, y, zl)

    def partner(ph):
        return pick(ph, me ^ 1, me ^ 2)

    def stage_copy(ph, unit):
        slot = lax.rem(unit, STAGE)
        line = 4 * unit + residue_of(ph, partner(ph))
        return pltpu.make_async_copy(spectra.at[:, :, line, :], stage.at[ph, slot], l_stage.at[ph, slot])

    def own_copy(q, par, e):
        ph = q // 8
        line = 4 * (2 * (q % 8) + e) + residue_of(ph, me)
        return pltpu.make_async_copy(spectra.at[:, :, line, :], own.at[par, e], l_own.at[par, e])

    for first in range(STAGE):
        for ph in range(2):
            stage_copy(ph, first).start()
    for e in range(2):
        own_copy(0, 0, e).start()

    barrier = pltpu.get_barrier_semaphore()
    for d in range(1, 8):
        pl.semaphore_signal(barrier, inc=1, device_id=(me ^ d, sta), device_id_type=MESH)
    for d in range(1, 4):
        pl.semaphore_signal(barrier, inc=1, device_id=(me, sta ^ d), device_id_type=MESH)
    for j in range(8):
        current_b[j // 4, j % 4] = current[j].astype(jnp.bfloat16)
    pl.semaphore_wait(barrier, 10)

    def x_remote(ph, fd, m, source, origin):
        return pltpu.make_async_remote_copy(
            current_b.at[:, residue_of(ph, fd), :, pl.ds(pl.multiple_of(16 * block_of(ph, fd, m), 16), 16), :],
            x_all.at[sta, pl.ds(8 * 2 * ph + 2 * origin, 2), :, pl.ds(16 * m, 16), :],
            x_send.at[ph, m, source], x_recv.at[ph, m, origin],
            device_id=(fd, sta), device_id_type=MESH,
        )

    def x_local(ph, m):
        return pltpu.make_async_copy(
            current_b.at[:, residue_of(ph, me), :, pl.ds(pl.multiple_of(16 * block_of(ph, me, m), 16), 16), :],
            x_all.at[sta, pl.ds(8 * 2 * ph + 2 * me, 2), :, pl.ds(16 * m, 16), :],
            x_recv.at[ph, m, me],
        )

    for ph in range(2):
        for m in range(2):
            x_local(ph, m).start()
        for d in range(1, 8):
            for m in range(2):
                x_remote(ph, me ^ d, m, d, me).start()

    def forward(ph, origin):
        for m in range(2):
            @pl.when(origin == me)
            def _():
                x_local(ph, m).wait()

            @pl.when(origin != me)
            def _():
                x_remote(ph, me, m, 1, origin).wait_recv()
        for d in range(1, 4):
            y_remote(ph, origin, d).start()

    def y_remote(ph, origin, d):
        rows = pl.ds(8 * 2 * ph + 2 * origin, 2)
        return pltpu.make_async_remote_copy(
            x_all.at[sta, rows], x_all.at[sta, rows],
            y_send.at[ph, origin, d], y_recv.at[ph, origin, d],
            device_id=(me, sta ^ d), device_id_type=MESH,
        )

    def s_remote(ph, unit):
        slot = lax.rem(unit, SBUF)
        return pltpu.make_async_remote_copy(
            sbuf.at[ph, slot], spec_rx.at[ph, unit], s_send.at[ph, slot], s_recv.at[ph, unit],
            device_id=(partner(ph), sta), device_id_type=MESH,
        )

    def send_unit(unit):
        for ph in range(2):
            stage_copy(ph, unit).wait()

            @pl.when(unit >= SBUF)
            def _():
                s_remote(ph, unit - SBUF).wait_send()

            sbuf[ph, lax.rem(unit, SBUF)] = stage[ph, lax.rem(unit, STAGE)].astype(jnp.bfloat16)
            s_remote(ph, unit).start()

            @pl.when(unit + STAGE < UNITS)
            def _():
                stage_copy(ph, unit + STAGE).start()

    tab_t[...] = jnp.transpose(jnp.bitwise_and(table[...], period - 1).astype(jnp.float32)).astype(jnp.bfloat16)
    slow_t[...] = jnp.transpose(slowness[...])
    cells = delay.shape[0]
    scale = 1.0 / period

    def strips():
        for r in range(0, cells, ROWS):
            for c in range(0, TILE, COLS):
                yield slice(r, r + ROWS), slice(c, c + COLS), slice(TILE + c, TILE + c + COLS)

    def start_chain(ph, unit, turn, cs, t, at):
        row, col, col_s = at
        second = twice(unit)
        if ph == 0:
            third = times(unit, second)
            a = jnp.where(y == 0, third[0], unit[0]), -jnp.where(y == 0, third[1], unit[1])
            b = jnp.where(y == 0, unit[0], third[0]), jnp.where(y == 0, unit[1], third[1])
        else:
            fourth = twice(second)
            a = jnp.where(zl == 0, second[0], 1.0), jnp.where(zl == 0, -second[1], 0.0)
            b = jnp.where(zl == 0, second[0], fourth[0]), jnp.where(zl == 0, second[1], fourth[1])
        store_pair(a, b, turn, cs, t, at, first=True)

    def store_pair(a, b, turn, cs, t, at, first):
        row, col, col_s = at
        one = b if first else (turn * b[0] - a[0], turn * b[1] - a[1])
        old = a if first else b
        two = turn * one[0] - old[0], turn * one[1] - old[1]
        prev_cos[t, row, col], prev_sin[t, row, col] = one
        now_cos[t, row, col], now_sin[t, row, col] = two
        for e, value in enumerate((one, two)):
            cs[e, t, row, col] = value[0].astype(jnp.bfloat16)
            cs[e, t, row, col_s] = value[1].astype(jnp.bfloat16)

    def angles(t, _):
        lanes = pl.ds(pl.multiple_of(t * TILE, TILE), TILE)
        picks = lax.broadcasted_iota(jnp.int32, (tab_t.shape[1], TILE), 0)
        picks = jnp.where(picks == blocks[:, lanes], 1.0, 0.0).astype(jnp.bfloat16)
        delay[...] = jnp.dot(tab_t[...], picks, preferred_element_type=jnp.float32)

        def strip(index, _):
            r = pl.multiple_of(index * ROWS, ROWS)
            row = pl.ds(r, ROWS)
            slow = slow_t[row, :]
            for c in range(0, TILE, COLS):
                col, col_s = slice(c, c + COLS), slice(TILE + c, TILE + c + COLS)
                here = pl.ds(pl.multiple_of(t * TILE + c, COLS), COLS)
                geometry = offsets[0:1, here] * slow[:, 0:1] + offsets[1:2, here] * slow[:, 1:2]
                turns = delay[row, col] * scale
                unit = turns_cos_sin((delay[row, col] + geometry) * scale)
                turns = 4.0 * turns
                fourth, _ = turns_cos_sin((turns - jnp.round(turns)) + geometry * (4.0 * scale))
                turn = fourth + fourth
                unit_cos[t, row, col], unit_sin[t, row, col] = unit
                chain[t, row, col] = turn
                start_chain(0, unit, turn, cs_a, t, (row, col, col_s))
            return 0

        lax.fori_loop(0, cells // ROWS, strip, 0)
        send_unit(t)
        return 0

    lax.fori_loop(0, tiles, angles, 0)

    def again(t, _):
        def strip(index, _):
            row = pl.ds(pl.multiple_of(index * ROWS, ROWS), ROWS)
            for c in range(0, TILE, COLS):
                col, col_s = slice(c, c + COLS), slice(TILE + c, TILE + c + COLS)
                unit = unit_cos[t, row, col], unit_sin[t, row, col]
                start_chain(1, unit, chain[t, row, col], cs_a, t, (row, col, col_s))
            return 0

        lax.fori_loop(0, cells // ROWS, strip, 0)
        return 0

    def forward_all(origin, _):
        forward(0, origin)
        return 0

    lax.fori_loop(0, 8, forward_all, 0)

    across = (((1,), (1,)), ((), ()))

    def g1_remote(q, par, k):
        share = 1 - core + 2 * k
        return pltpu.make_async_remote_copy(
            gbuf.at[par, share], rx1.at[lax.rem(q, 4), k], g1_send.at[par, k], g1_recv.at[lax.rem(q, 4), k],
            device_id=(me, sta ^ 1), device_id_type=MESH,
        )

    def g2_remote(q, par):
        return pltpu.make_async_remote_copy(
            tx2.at[par], rx2.at[lax.rem(q, 4)], g2_send.at[par], g2_recv.at[lax.rem(q, 4)],
            device_id=(me, sta ^ 2), device_id_type=MESH,
        )

    def g3_remote(q, par, m, target):
        ph = q // 8
        return pltpu.make_async_remote_copy(
            tx3.at[par, :, :, m],
            home.at[:, residue_of(ph, me), :, pl.ds(pl.multiple_of(16 * block_of(ph, me, m), 16), 16), :],
            g3_send.at[par, m], g3_recv.at[ph, m, me],
            device_id=(target, sta), device_id_type=MESH,
        )

    def g3_local(q, par, m):
        ph = q // 8
        return pltpu.make_async_copy(
            tx3.at[par, :, :, m],
            home.at[:, residue_of(ph, me), :, pl.ds(pl.multiple_of(16 * block_of(ph, me, m), 16), 16), :],
            g3_recv.at[ph, m, me],
        )

    def g3_arrived(ph, m, origin):
        return pltpu.make_async_remote_copy(
            tx3.at[0, :, :, m],
            home.at[:, residue_of(ph, origin), :, pl.ds(pl.multiple_of(16 * block_of(ph, origin, m), 16), 16), :],
            g3_send.at[0, m], g3_recv.at[ph, m, origin],
            device_id=(me, sta), device_id_type=MESH,
        )

    def stage1(q, par):
        for k in range(2):
            g1_remote(q, par, k).start()

    def stage2(q, par):
        for k in range(2):
            g1_remote(q, par, k).wait()

        @pl.when(q >= 2)
        def _():
            g2_remote(q - 2, par).wait_send()

        slot = lax.rem(q, 4)
        tx2[par] = gbuf[par, core + 2 * (1 - x)] + rx1[slot, 1 - x]
        keep2[par] = gbuf[par, core + 2 * x] + rx1[slot, x]
        g2_remote(q, par).start()

    def stage3(q, par):
        g2_remote(q, par).wait_recv()

        @pl.when(q >= 2)
        def _():
            finish3(q - 2, par)

        total = (keep2[par] + rx2[lax.rem(q, 4)]) * normalizer
        tx3[par] = total.reshape(tx3.shape[1:])
        target = lax.rem(q, 8)

        @pl.when(target == me)
        def _():
            for m in range(2):
                g3_local(q, par, m).start()

        @pl.when(target != me)
        def _():
            for m in range(2):
                g3_remote(q, par, m, target).start()

    def finish3(q, par):
        @pl.when(lax.rem(q, 8) == me)
        def _():
            for m in range(2):
                g3_local(q, par, m).wait()

        @pl.when(lax.rem(q, 8) != me)
        def _():
            for m in range(2):
                g3_remote(q, par, m, lax.rem(q, 8)).wait_send()

    def run_pair(q, par, cs, cs_next):
        ph, p = q // 8, lax.rem(q, 8)
        mem = member(ph)

        for e in range(2):
            @pl.when(q < 15)
            def _():
                own_copy(q + 1, 1 - par, e).start()

        @pl.when(4 + 2 * q < UNITS)
        def _():
            for k in range(2):
                send_unit(4 + 2 * q + k)

        for d in range(1, 4):
            y_remote(ph, p, d).wait_recv()
        for e in range(2):
            s_remote(ph, 2 * p + e).wait_recv()
            own_copy(q, par, e).wait()
        gbuf[par] = jnp.zeros_like(gbuf[par])

        def body(t, _):
            lanes = pl.ds(pl.multiple_of(t * TILE, TILE), TILE)
            rcats = []
            for e in range(2):
                at = 2 * q + e
                x1 = jnp.concatenate([x_all[s, at].reshape(64, 128) for s in range(4)], axis=1)
                x2 = jnp.concatenate([x1[32:], -x1[:32]], axis=0)
                both = jnp.concatenate([x1, x2], axis=1)
                acc = jnp.dot(x1, cs[e, t, :, 0:TILE], preferred_element_type=jnp.float32)
                acc += jnp.dot(x2, cs[e, t, :, TILE:], preferred_element_type=jnp.float32)
                acc = acc * normalizer
                seen = []
                for k in range(2):
                    mine = own[par, e, k, :, lanes]
                    theirs = spec_rx[ph, 2 * p + e, k, :, lanes].astype(jnp.float32)
                    seen.append(jnp.where(mem == 0, mine, theirs))
                    seen.append(jnp.where(mem == 0, theirs, mine))
                res = (acc - jnp.concatenate(seen, axis=0)).astype(jnp.bfloat16)
                rcats.append(jnp.concatenate([res, jnp.concatenate([-res[32:], res[:32]], axis=0)], axis=1))
            for e in range(2):
                back = lax.dot_general(rcats[e], cs[e, t], across, preferred_element_type=jnp.float32)
                for s in range(4):
                    gbuf[par, s, 64 * e : 64 * e + 64, :] += back[:, 128 * s : 128 * s + 128]
            for at in strips():
                row, col, _ = at
                store_pair(
                    (prev_cos[t, row, col], prev_sin[t, row, col]),
                    (now_cos[t, row, col], now_sin[t, row, col]),
                    chain[t, row, col], cs_next, t, at, first=False,
                )
            return 0

        lax.fori_loop(0, tiles, body, 0)

        @pl.when(q < 8)
        def _():
            forward(1, p)

        stage1(q, par)

        @pl.when(q >= 1)
        def _():
            stage2(q - 1, 1 - par)

        @pl.when(q >= 2)
        def _():
            stage3(q - 2, par)

    def two_pairs(i, _):
        run_pair(2 * i, 0, cs_a, cs_b)
        run_pair(2 * i + 1, 1, cs_b, cs_a)

        @pl.when(i == 3)
        def _():
            lax.fori_loop(0, tiles, again, 0)

        return 0

    lax.fori_loop(0, 8, two_pairs, 0)
    stage2(15, 1)
    stage3(14, 0)
    stage3(15, 1)

    for ph in range(2):
        for d in range(1, 8):
            for m in range(2):
                x_remote(ph, me ^ d, m, d, me).wait_send()
        for unit in range(UNITS - SBUF, UNITS):
            s_remote(ph, unit).wait_send()
    for ph in range(2):
        def left(origin, _):
            for d in range(1, 4):
                y_remote(ph, origin, d).wait_send()
            return 0

        lax.fori_loop(0, 8, left, 0)
    g2_remote(14, 0).wait_send()
    g2_remote(15, 1).wait_send()

    finish3(14, 0)
    finish3(15, 1)
    for ph in range(2):
        for d in range(1, 8):
            for m in range(2):
                g3_arrived(ph, m, me ^ d).wait_recv()

    def step_block(w, _):
        rows = pl.ds(pl.multiple_of(w * 16, 16), 16)
        total = jnp.zeros((16, 128), jnp.float32)
        for j in range(8):
            for k in range(2):
                value = current[j, k, rows, :] - step_size * home[j // 4, j % 4, k, rows, :]
                stepped_out[j, k, rows, :] = value
                total = total + value * value
        sums[0, w] = total
        return 0

    lax.fori_loop(0, 8, step_block, 0)

    def n_remote(d):
        return pltpu.make_async_remote_copy(
            sums.at[0, me ^ d], sums.at[1, d], n_send.at[d], n_recv.at[d],
            device_id=(me ^ d, sta), device_id_type=MESH,
        )

    for d in range(1, 8):
        n_remote(d).start()
    total = sums[0, me]
    for d in range(1, 8):
        n_remote(d).wait()
        total = total + sums[1, d]
    group_norm = jnp.sqrt(total + 1e-06)
    shrinks[me] = jnp.maximum(0.0, 1.0 - step_size * weights[...] / group_norm)

    def m_remote(d, slot):
        return pltpu.make_async_remote_copy(
            shrinks.at[slot], shrinks.at[slot], m_send.at[d], m_recv.at[d],
            device_id=(me ^ d, sta), device_id_type=MESH,
        )

    for d in range(1, 8):
        m_remote(d, me).start()
    for d in range(1, 8):
        m_remote(d, me).wait_send()
        m_remote(d, me ^ d).wait_recv()
    shrink_out[...] = shrinks[...].reshape(shrink_out.shape)


def local_paired(freq_size, sta_size, spectra, current, previous, table, station_block, offsets, slowness, weights, momentum):
    period = 4 * F
    normalizer = 1.0 / math.sqrt(CELLS)
    bins, _, windows, share = current.shape
    stations = station_block.shape[0]
    cells = table.shape[1]
    step_size = CELLS / (math.sqrt(stations * sta_size) + math.sqrt(CELLS)) ** 2
    tiles = stations // TILE
    f32, bf16 = jnp.float32, jnp.bfloat16
    vm, dma = pltpu.VMEM, pltpu.SemaphoreType.DMA
    state = vm((tiles, cells, TILE), f32)
    piece = spectra.shape[1]
    slow = jnp.pad(slowness, ((0, 6), (0, 0)))
    inside = pl.BlockSpec(memory_space=pltpu.VMEM)
    stepped, shrink = pl.pallas_call(
        functools.partial(iteration_kernel, period, normalizer, step_size),
        out_shape=(
            jax.ShapeDtypeStruct((bins, 2, windows, share), f32),
            jax.ShapeDtypeStruct((windows, share), f32),
        ),
        in_specs=[pl.BlockSpec(memory_space=pl.ANY)] + [inside] * 6,
        out_specs=(inside, inside),
        scratch_shapes=[
            vm((2, tiles, cells, 2 * TILE), bf16),
            vm((2, tiles, cells, 2 * TILE), bf16),
            state, state, state, state, state, state, state,
            vm((cells, table.shape[0]), bf16),
            vm((cells, 8), f32),
            vm((cells, TILE), f32),
            vm((2, 4, 2, windows, share), bf16),
            vm((4, 32, 2, 32, share), bf16),
            vm((2, UNITS, 2, piece, stations), bf16),
            vm((2, SBUF, 2, piece, stations), bf16),
            vm((2, STAGE, 2, piece, stations), f32),
            vm((2, 2, 2, piece, stations), f32),
            vm((2, 4, 2, windows, share), f32),
            vm((2, 4, 128, share), f32),
            vm((4, 2, 128, share), f32),
            vm((4, 128, share), f32),
            vm((2, 128, share), f32),
            vm((2, 128, share), f32),
            vm((2, 2, 2, 2, 16, share), f32),
            vm((2, 8, 16, share), f32),
            vm((8, 16, share), f32),
            dma((2, 2, 8)), dma((2, 2, 8)), dma((2, 8, 4)), dma((2, 8, 4)),
            dma((2, SBUF)), dma((2, UNITS)), dma((2, STAGE)), dma((2, 2)),
            dma((2, 2)), dma((4, 2)), dma((2,)), dma((4,)), dma((2, 2)), dma((2, 2, 8)),
            dma((8,)), dma((8,)), dma((8,)), dma((8,)),
        ],
        compiler_params=pltpu.CompilerParams(
            vmem_limit_bytes=63 * 2**20, collective_id=0, has_side_effects=True
        ),
        cost_estimate=pl.CostEstimate(
            flops=8 * 32 * 64 * cells * stations, bytes_accessed=24 * 2**20, transcendentals=0
        ),
    )(spectra, current, table, station_block.reshape(1, -1), offsets, slow, weights.reshape(1, -1))
    estimate = stepped * shrink
    momentum_now = momentum[0]
    momentum_next = (1.0 + jnp.sqrt(1.0 + 4.0 * momentum_now * momentum_now)) / 2.0
    extrapolated = estimate + (momentum_now - 1.0) / momentum_next * (estimate - previous)
    return (estimate, extrapolated)


def solution(mesh):
    freq_size, sta_size = mesh.shape["freq"], mesh.shape["sta"]
    body = local
    if freq_size == 8 and sta_size == 4:
        body = functools.partial(local_paired, freq_size, sta_size)
    in_specs = (
        P(None, "freq", None, "sta"),
        P("freq", None, None, "sta"),
        P("freq", None, None, "sta"),
        P(),
        P("sta"),
        P(None, "sta"),
        P(),
        P("sta"),
        P(),
    )
    out_specs = (P("freq", None, None, "sta"), P("freq", None, None, "sta"))
    return jax.shard_map(body, mesh=mesh, in_specs=in_specs, out_specs=out_specs, check_vma=False)
```

time: 237 us -> 168 us (0.71)
  Pallas kernels: 91.5 us -> 162 us
  waiting for transfers between devices: 48.9 us -> 0 us
  starting transfers between devices: 37.6 us -> 0 us
  local copies, waits for them, and re-layouts: 31.3 us -> 1.3 us
  between operations: 14.9 us -> 1.37 us
  other arithmetic: 12.6 us -> 3.16 us
    pallas_call x3 -> x1, Pallas kernels: 91.5 us -> 162 us  [local_paired(): pl.pallas_call(functools.partial(iteration_kernel, period, normalizer, st...]
    ppermute x19 -> x0, waiting for transfers between devices: 48.9 us -> none  [the longest x6 20.5 us: local_grouped(): lax.ppermute(parts[d], 'freq', [(f, f ^ d) for f in range(freq_size)])]
    ppermute x19 -> x0, starting transfers between devices: 37.6 us -> none  [the longest x3 17.1 us: local_grouped(): lax.ppermute(squares, 'freq', [(f, f ^ d) for f in range(freq_size)])]
    dynamic_slice x4 -> x0, local copies, waits for them, and re-layouts: 14.3 us -> none  [the longest x1 8.82 us: local_grouped(): lax.dynamic_slice_in_dim(spectra, first, bins, 2).astype(jnp.bfloat16)]
    unnamed x32 -> x0, local copies, waits for them, and re-layouts: 8.51 us -> none
    transpose x2 -> x0, local copies, waits for them, and re-layouts: 6.72 us -> none  [local_grouped(): parts.append(jnp.transpose(part, (2, 0, 1, 3)))]
    mul x3 -> x0, other arithmetic: 3.24 us -> none  [the longest x2 3.23 us: local_grouped(): home = lax.ppermute(total * normalizer, 'freq', gradient_back[c])]
  transfers between devices with their start and end apart: 20 -> 0, of which waited for: 10 -> 0; matrix products, arithmetic and copies ran while one was open for 15% -> 0% of each run, Pallas kernels for 39% -> 0%
where the time goes in v1:
time: 168 us; the launch traced here: 167 us
  Pallas kernels  162 us (96%)
  other arithmetic  3.16 us (2%)
    pallas_call x1, Pallas kernels, local_paired(): pl.pallas_call(functools.partial(iteration_kernel, period, normalizer, st...  162 us

profile of v1, /device:TPU:0, one launch (start us, length us, event | category | flops | bytes accessed | tf_op | source)
XLA Modules:
  0.0 167.4 jit_solution(13459472157144450063)
XLA Ops:
  1.4 1.3 pad.4.slowness
  2.7 161.6 %shard_map.104 = (f32[8,2,128,128]{3,2,1,0:T(8,128)}, f32[128,128]{1,0:T(8,128)}) custom-call(f32[2,16,64,2048]{3,2,1,0:T(8,128)} %spectra.1, f32[8,2,128,128]{3,2,1,0:T(8,128)} %current.1, s32[64,512]{1,0:T(8,128)} %table.1, s32[1,2048]{1,0:T(1,128)} %bitcast.6, f32[2,2048]{1,0:T(2,128)} %offsets.1, f32[8,512]{1,0:T(8,128)} %pad.4.slowness, f32[1,128]{1,0:T(1,128)} %bitcast.7), custom_call_target="tpu_custom_call" | custom-call | flops 17179869184 | bytes 25165824 | tf_op jit(solution)/shard_map/pallas_call | solution.py:600
  164.2 3.2 %multiply_add_fusion = (f32[8,2,128,128]{3,2,1,0:T(8,128)}, f32[8,2,128,128]{3,2,1,0:T(8,128)}) fusion(f32[8,2,128,128]{3,2,1,0:T(8,128)} %param.11, f32[]{:T(128)S(6)} %div.7, f32[8,2,128,128]{3,2,1,0:T(8,128)} %get-tuple-element.4, f32[128,128]{1,0:T(8,128)} %get-tuple-element.5), kind=kLoop, calls=%fused_computation | loop fusion | flops 1048576 | bytes 4259844 | tf_op jit(solution)/shard_map/add | solution.py:645

commit v2 on v1

--- a/solution.py
+++ b/solution.py
@@ -113,6 +113,7 @@
 ROWS = 32
 COLS = 256
 UNITS = 16
+STRIP = 16
 SBUF = 4
 STAGE = 2
 
@@ -144,13 +145,13 @@
 
 def iteration_kernel(
     period, normalizer, step_size,
-    spectra, current, table, blocks, offsets, slowness, weights,
+    spectra, current_in, table, blocks, offsets, slowness, weights,
     stepped_out, shrink_out,
     cs_a, cs_b, prev_cos, prev_sin, now_cos, now_sin, unit_cos, unit_sin, chain,
-    tab_t, slow_t, delay,
+    tab_t, slow_8, slow_t, delay, current,
     current_b, x_all, spec_rx, sbuf, stage, own, home, gbuf, rx1, rx2, tx2, keep2, tx3, sums, shrinks,
     x_send, x_recv, y_send, y_recv, s_send, s_recv, l_stage, l_own,
-    g1_send, g1_recv, g2_send, g2_recv, g3_send, g3_recv, n_send, n_recv, m_send, m_recv,
+    g1_send, g1_recv, g2_send, g2_recv, g3_send, g3_recv, n_send, n_recv, m_send, m_recv, l_current,
 ):
     me = lax.axis_index("freq")
     sta = lax.axis_index("sta")
@@ -184,17 +185,19 @@
         line = 4 * (2 * (q % 8) + e) + residue_of(ph, me)
         return pltpu.make_async_copy(spectra.at[:, :, line, :], own.at[par, e], l_own.at[par, e])
 
+    load = pltpu.make_async_copy(current_in, current, l_current)
+    load.start()
+    barrier = pltpu.get_barrier_semaphore()
+    for d in range(1, 8):
+        pl.semaphore_signal(barrier, inc=1, device_id=(me ^ d, sta), device_id_type=MESH)
+    for d in range(1, 4):
+        pl.semaphore_signal(barrier, inc=1, device_id=(me, sta ^ d), device_id_type=MESH)
+    load.wait()
     for first in range(STAGE):
         for ph in range(2):
             stage_copy(ph, first).start()
     for e in range(2):
         own_copy(0, 0, e).start()
-
-    barrier = pltpu.get_barrier_semaphore()
-    for d in range(1, 8):
-        pl.semaphore_signal(barrier, inc=1, device_id=(me ^ d, sta), device_id_type=MESH)
-    for d in range(1, 4):
-        pl.semaphore_signal(barrier, inc=1, device_id=(me, sta ^ d), device_id_type=MESH)
     for j in range(8):
         current_b[j // 4, j % 4] = current[j].astype(jnp.bfloat16)
     pl.semaphore_wait(barrier, 10)
@@ -230,16 +233,22 @@
             @pl.when(origin != me)
             def _():
                 x_remote(ph, me, m, 1, origin).wait_recv()
-        for d in range(1, 4):
+        for d in range(1, 3):
             y_remote(ph, origin, d).start()
 
     def y_remote(ph, origin, d):
-        rows = pl.ds(8 * 2 * ph + 2 * origin, 2)
-        return pltpu.make_async_remote_copy(
-            x_all.at[sta, rows], x_all.at[sta, rows],
+        rows = pl.ds(16 * ph + 2 * origin, 2)
+        held = sta ^ 2 if d == 3 else sta
+        return pltpu.make_async_remote_copy(
+            x_all.at[held, rows], x_all.at[held, rows],
             y_send.at[ph, origin, d], y_recv.at[ph, origin, d],
-            device_id=(me, sta ^ d), device_id_type=MESH,
-        )
+            device_id=(me, sta ^ (2 if d == 2 else 1)), device_id_type=MESH,
+        )
+
+    def relay(q):
+        ph, origin = q // 8, lax.rem(q, 8)
+        y_remote(ph, origin, 2).wait_recv()
+        y_remote(ph, origin, 3).start()
 
     def s_remote(ph, unit):
         slot = lax.rem(unit, SBUF)
@@ -248,33 +257,28 @@
             device_id=(partner(ph), sta), device_id_type=MESH,
         )
 
-    def send_unit(unit):
-        for ph in range(2):
-            stage_copy(ph, unit).wait()
-
-            @pl.when(unit >= SBUF)
-            def _():
-                s_remote(ph, unit - SBUF).wait_send()
-
-            sbuf[ph, lax.rem(unit, SBUF)] = stage[ph, lax.rem(unit, STAGE)].astype(jnp.bfloat16)
-            s_remote(ph, unit).start()
-
-            @pl.when(unit + STAGE < UNITS)
-            def _():
-                stage_copy(ph, unit + STAGE).start()
+    def send_unit(ph, unit):
+        stage_copy(ph, unit).wait()
+
+        @pl.when(unit >= SBUF)
+        def _():
+            s_remote(ph, unit - SBUF).wait_send()
+
+        sbuf[ph, lax.rem(unit, SBUF)] = stage[ph, lax.rem(unit, STAGE)].astype(jnp.bfloat16)
+        s_remote(ph, unit).start()
+
+        @pl.when(unit + STAGE < UNITS)
+        def _():
+            stage_copy(ph, unit + STAGE).start()
 
     tab_t[...] = jnp.transpose(jnp.bitwise_and(table[...], period - 1).astype(jnp.float32)).astype(jnp.bfloat16)
-    slow_t[...] = jnp.transpose(slowness[...])
+    slow_8[...] = jnp.zeros_like(slow_8)
+    slow_8[0:2, :] = slowness[...]
+    slow_t[...] = jnp.transpose(slow_8[...])
     cells = delay.shape[0]
     scale = 1.0 / period
 
-    def strips():
-        for r in range(0, cells, ROWS):
-            for c in range(0, TILE, COLS):
-                yield slice(r, r + ROWS), slice(c, c + COLS), slice(TILE + c, TILE + c + COLS)
-
     def start_chain(ph, unit, turn, cs, t, at):
-        row, col, col_s = at
         second = twice(unit)
         if ph == 0:
             third = times(unit, second)
@@ -284,7 +288,7 @@
             fourth = twice(second)
             a = jnp.where(zl == 0, second[0], 1.0), jnp.where(zl == 0, -second[1], 0.0)
             b = jnp.where(zl == 0, second[0], fourth[0]), jnp.where(zl == 0, second[1], fourth[1])
-        store_pair(a, b, turn, cs, t, at, first=True)
+        return store_pair(a, b, turn, cs, t, at, True)
 
     def store_pair(a, b, turn, cs, t, at, first):
         row, col, col_s = at
@@ -296,6 +300,28 @@
         for e, value in enumerate((one, two)):
             cs[e, t, row, col] = value[0].astype(jnp.bfloat16)
             cs[e, t, row, col_s] = value[1].astype(jnp.bfloat16)
+        return two[0]
+
+    def fill(cs, t, fresh):
+        after = None
+        for r in range(0, cells, STRIP):
+            for c in range(0, TILE, 128):
+                row, col, col_s = slice(r, r + STRIP), slice(c, c + 128), slice(TILE + c, TILE + c + 128)
+                turn = chain[t, row, col]
+                if after is not None:
+                    turn = turn + after
+                at = row, col, col_s
+                if fresh:
+                    unit = unit_cos[t, row, col], unit_sin[t, row, col]
+                    if after is not None:
+                        unit = unit[0] + after, unit[1]
+                    last = start_chain(1, unit, turn, cs, t, at)
+                else:
+                    old = prev_cos[t, row, col], prev_sin[t, row, col]
+                    now = now_cos[t, row, col], now_sin[t, row, col]
+                    last = store_pair(old, now, turn, cs, t, at, False)
+                zero = jnp.minimum(jnp.maximum(last[0:8], 0.0), 0.0)
+                after = jnp.concatenate([zero] * (STRIP // 8), axis=0)
 
     def angles(t, _):
         lanes = pl.ds(pl.multiple_of(t * TILE, TILE), TILE)
@@ -322,28 +348,16 @@
             return 0
 
         lax.fori_loop(0, cells // ROWS, strip, 0)
-        send_unit(t)
+        send_unit(0, t)
+
+        @pl.when(t >= 2)
+        def _():
+            for k in range(4):
+                forward(0, 4 * (t - 2) + k)
+
         return 0
 
     lax.fori_loop(0, tiles, angles, 0)
-
-    def again(t, _):
-        def strip(index, _):
-            row = pl.ds(pl.multiple_of(index * ROWS, ROWS), ROWS)
-            for c in range(0, TILE, COLS):
-                col, col_s = slice(c, c + COLS), slice(TILE + c, TILE + c + COLS)
-                unit = unit_cos[t, row, col], unit_sin[t, row, col]
-                start_chain(1, unit, chain[t, row, col], cs_a, t, (row, col, col_s))
-            return 0
-
-        lax.fori_loop(0, cells // ROWS, strip, 0)
-        return 0
-
-    def forward_all(origin, _):
-        forward(0, origin)
-        return 0
-
-    lax.fori_loop(0, 8, forward_all, 0)
 
     across = (((1,), (1,)), ((), ()))
 
@@ -360,19 +374,19 @@
             device_id=(me, sta ^ 2), device_id_type=MESH,
         )
 
-    def g3_remote(q, par, m, target):
+    def g3_remote(q, m, target):
         ph = q // 8
         return pltpu.make_async_remote_copy(
-            tx3.at[par, :, :, m],
+            tx3.at[lax.rem(q, 8), :, :, m],
             home.at[:, residue_of(ph, me), :, pl.ds(pl.multiple_of(16 * block_of(ph, me, m), 16), 16), :],
-            g3_send.at[par, m], g3_recv.at[ph, m, me],
+            g3_send.at[lax.rem(q, 8), m], g3_recv.at[ph, m, me],
             device_id=(target, sta), device_id_type=MESH,
         )
 
-    def g3_local(q, par, m):
+    def g3_local(q, m):
         ph = q // 8
         return pltpu.make_async_copy(
-            tx3.at[par, :, :, m],
+            tx3.at[lax.rem(q, 8), :, :, m],
             home.at[:, residue_of(ph, me), :, pl.ds(pl.multiple_of(16 * block_of(ph, me, m), 16), 16), :],
             g3_recv.at[ph, m, me],
         )
@@ -405,34 +419,34 @@
     def stage3(q, par):
         g2_remote(q, par).wait_recv()
 
-        @pl.when(q >= 2)
-        def _():
-            finish3(q - 2, par)
+        @pl.when(q >= 8)
+        def _():
+            finish3(q - 8)
 
         total = (keep2[par] + rx2[lax.rem(q, 4)]) * normalizer
-        tx3[par] = total.reshape(tx3.shape[1:])
         target = lax.rem(q, 8)
+        tx3[target] = total.reshape(tx3.shape[1:])
 
         @pl.when(target == me)
         def _():
             for m in range(2):
-                g3_local(q, par, m).start()
+                g3_local(q, m).start()
 
         @pl.when(target != me)
         def _():
             for m in range(2):
-                g3_remote(q, par, m, target).start()
-
-    def finish3(q, par):
+                g3_remote(q, m, target).start()
+
+    def finish3(q):
         @pl.when(lax.rem(q, 8) == me)
         def _():
             for m in range(2):
-                g3_local(q, par, m).wait()
+                g3_local(q, m).wait()
 
         @pl.when(lax.rem(q, 8) != me)
         def _():
             for m in range(2):
-                g3_remote(q, par, m, lax.rem(q, 8)).wait_send()
+                g3_remote(q, m, lax.rem(q, 8)).wait_send()
 
     def run_pair(q, par, cs, cs_next):
         ph, p = q // 8, lax.rem(q, 8)
@@ -446,23 +460,31 @@
         @pl.when(4 + 2 * q < UNITS)
         def _():
             for k in range(2):
-                send_unit(4 + 2 * q + k)
-
-        for d in range(1, 4):
-            y_remote(ph, p, d).wait_recv()
+                send_unit(0, 4 + 2 * q + k)
+
+        @pl.when(2 * q < UNITS)
+        def _():
+            for k in range(2):
+                send_unit(1, 2 * q + k)
+
+        @pl.when(q < 15)
+        def _():
+            relay(q + 1)
+
+        y_remote(ph, p, 1).wait_recv()
+        y_remote(ph, p, 3).wait_recv()
         for e in range(2):
             s_remote(ph, 2 * p + e).wait_recv()
             own_copy(q, par, e).wait()
         gbuf[par] = jnp.zeros_like(gbuf[par])
 
-        def body(t, _):
+        def body(mode, t, _):
             lanes = pl.ds(pl.multiple_of(t * TILE, TILE), TILE)
             rcats = []
             for e in range(2):
                 at = 2 * q + e
                 x1 = jnp.concatenate([x_all[s, at].reshape(64, 128) for s in range(4)], axis=1)
                 x2 = jnp.concatenate([x1[32:], -x1[:32]], axis=0)
-                both = jnp.concatenate([x1, x2], axis=1)
                 acc = jnp.dot(x1, cs[e, t, :, 0:TILE], preferred_element_type=jnp.float32)
                 acc += jnp.dot(x2, cs[e, t, :, TILE:], preferred_element_type=jnp.float32)
                 acc = acc * normalizer
@@ -478,16 +500,17 @@
                 back = lax.dot_general(rcats[e], cs[e, t], across, preferred_element_type=jnp.float32)
                 for s in range(4):
                     gbuf[par, s, 64 * e : 64 * e + 64, :] += back[:, 128 * s : 128 * s + 128]
-            for at in strips():
-                row, col, _ = at
-                store_pair(
-                    (prev_cos[t, row, col], prev_sin[t, row, col]),
-                    (now_cos[t, row, col], now_sin[t, row, col]),
-                    chain[t, row, col], cs_next, t, at, first=False,
-                )
+            if mode != "none":
+                fill(cs_next, t, mode == "fresh")
             return 0
 
-        lax.fori_loop(0, tiles, body, 0)
+        if par == 0:
+            lax.fori_loop(0, tiles, functools.partial(body, "next"), 0)
+        else:
+            for mode, here in (("fresh", q == 7), ("none", q == 15), ("next", (q != 7) & (q != 15))):
+                @pl.when(here)
+                def _():
+                    lax.fori_loop(0, tiles, functools.partial(body, mode), 0)
 
         @pl.when(q < 8)
         def _():
@@ -506,13 +529,9 @@
     def two_pairs(i, _):
         run_pair(2 * i, 0, cs_a, cs_b)
         run_pair(2 * i + 1, 1, cs_b, cs_a)
-
-        @pl.when(i == 3)
-        def _():
-            lax.fori_loop(0, tiles, again, 0)
-
         return 0
 
+    relay(0)
     lax.fori_loop(0, 8, two_pairs, 0)
     stage2(15, 1)
     stage3(14, 0)
@@ -534,8 +553,11 @@
     g2_remote(14, 0).wait_send()
     g2_remote(15, 1).wait_send()
 
-    finish3(14, 0)
-    finish3(15, 1)
+    def finished(q, _):
+        finish3(q)
+        return 0
+
+    lax.fori_loop(8, 16, finished, 0)
     for ph in range(2):
         for d in range(1, 8):
             for m in range(2):
@@ -595,7 +617,6 @@
     vm, dma = pltpu.VMEM, pltpu.SemaphoreType.DMA
     state = vm((tiles, cells, TILE), f32)
     piece = spectra.shape[1]
-    slow = jnp.pad(slowness, ((0, 6), (0, 0)))
     inside = pl.BlockSpec(memory_space=pltpu.VMEM)
     stepped, shrink = pl.pallas_call(
         functools.partial(iteration_kernel, period, normalizer, step_size),
@@ -603,15 +624,17 @@
             jax.ShapeDtypeStruct((bins, 2, windows, share), f32),
             jax.ShapeDtypeStruct((windows, share), f32),
         ),
-        in_specs=[pl.BlockSpec(memory_space=pl.ANY)] + [inside] * 6,
+        in_specs=[pl.BlockSpec(memory_space=pl.ANY)] * 2 + [inside] * 5,
         out_specs=(inside, inside),
         scratch_shapes=[
             vm((2, tiles, cells, 2 * TILE), bf16),
             vm((2, tiles, cells, 2 * TILE), bf16),
             state, state, state, state, state, state, state,
             vm((cells, table.shape[0]), bf16),
+            vm((8, cells), f32),
             vm((cells, 8), f32),
             vm((cells, TILE), f32),
+            vm(current.shape, f32),
             vm((2, 4, 2, windows, share), bf16),
             vm((4, 32, 2, 32, share), bf16),
             vm((2, UNITS, 2, piece, stations), bf16),
@@ -624,13 +647,13 @@
             vm((4, 128, share), f32),
             vm((2, 128, share), f32),
             vm((2, 128, share), f32),
-            vm((2, 2, 2, 2, 16, share), f32),
+            vm((8, 2, 2, 2, 16, share), f32),
             vm((2, 8, 16, share), f32),
             vm((8, 16, share), f32),
             dma((2, 2, 8)), dma((2, 2, 8)), dma((2, 8, 4)), dma((2, 8, 4)),
             dma((2, SBUF)), dma((2, UNITS)), dma((2, STAGE)), dma((2, 2)),
-            dma((2, 2)), dma((4, 2)), dma((2,)), dma((4,)), dma((2, 2)), dma((2, 2, 8)),
-            dma((8,)), dma((8,)), dma((8,)), dma((8,)),
+            dma((2, 2)), dma((4, 2)), dma((2,)), dma((4,)), dma((8, 2)), dma((2, 2, 8)),
+            dma((8,)), dma((8,)), dma((8,)), dma((8,)), dma(()),
         ],
         compiler_params=pltpu.CompilerParams(
             vmem_limit_bytes=63 * 2**20, collective_id=0, has_side_effects=True
@@ -638,7 +661,7 @@
         cost_estimate=pl.CostEstimate(
             flops=8 * 32 * 64 * cells * stations, bytes_accessed=24 * 2**20, transcendentals=0
         ),
-    )(spectra, current, table, station_block.reshape(1, -1), offsets, slow, weights.reshape(1, -1))
+    )(spectra, current, table, station_block.reshape(1, -1), offsets, slowness, weights.reshape(1, -1))
     estimate = stepped * shrink
     momentum_now = momentum[0]
     momentum_next = (1.0 + jnp.sqrt(1.0 + 4.0 * momentum_now * momentum_now)) / 2.0

time: 168 us -> 141 us (0.84)
  Pallas kernels: 162 us -> 136 us
    pallas_call x1, Pallas kernels: 162 us -> 136 us  [local_paired(): pl.pallas_call(functools.partial(iteration_kernel, period, normalizer, st...]
where the time goes in v2:
time: 141 us
  Pallas kernels  136 us (96%)
  other arithmetic  3.16 us (2%)
    pallas_call x1, Pallas kernels, local_paired(): pl.pallas_call(functools.partial(iteration_kernel, period, normalizer, st...  136 us
    add x1, other arithmetic, local_paired(): estimate + (momentum_now - 1.0) / momentum_next * (estimate - previous)  3.16 us

profile of v2, /device:TPU:0, one launch (start us, length us, event | category | flops | bytes accessed | tf_op | source)
XLA Modules:
  0.0 141.0 jit_solution(17286007530846176586)
XLA Ops:
  1.4 136.5 %shard_map.104 = (f32[8,2,128,128]{3,2,1,0:T(8,128)}, f32[128,128]{1,0:T(8,128)}) custom-call(f32[2,16,64,2048]{3,2,1,0:T(8,128)} %spectra.1, f32[8,2,128,128]{3,2,1,0:T(8,128)} %current_in.1, s32[64,512]{1,0:T(8,128)} %table.1, s32[1,2048]{1,0:T(1,128)} %bitcast.6, f32[2,2048]{1,0:T(2,128)} %offsets.1, f32[2,512]{1,0:T(2,128)} %slowness.1, f32[1,128]{1,0:T(1,128)} %bitcast.7), custom_call_target="tpu_custom_call" | custom-call | flops 17179869184 | bytes 25165824 | tf_op jit(solution)/shard_map/pallas_call | solution.py:621
  137.8 3.2 %multiply_add_fusion = (f32[8,2,128,128]{3,2,1,0:T(8,128)}, f32[8,2,128,128]{3,2,1,0:T(8,128)}) fusion(f32[8,2,128,128]{3,2,1,0:T(8,128)} %param.11, f32[]{:T(128)S(6)} %div.7, f32[8,2,128,128]{3,2,1,0:T(8,128)} %get-tuple-element.4, f32[128,128]{1,0:T(8,128)} %get-tuple-element.5), kind=kLoop, calls=%fused_computation | loop fusion | flops 1048576 | bytes 4259844 | tf_op jit(solution)/shard_map/add | solution.py:668

commit v3 on v2

--- a/solution.py
+++ b/solution.py
@@ -347,7 +347,7 @@
                 start_chain(0, unit, turn, cs_a, t, (row, col, col_s))
             return 0
 
-        lax.fori_loop(0, cells // ROWS, strip, 0)
+        lax.fori_loop(0, cells // ROWS, strip, 0, unroll=4)
         send_unit(0, t)
 
         @pl.when(t >= 2)

time: 141 us -> 138 us (0.979)
  Pallas kernels: 136 us -> 134 us
    pallas_call x1, Pallas kernels: 136 us -> 134 us  [local_paired(): pl.pallas_call(functools.partial(iteration_kernel, period, normalizer, st...]
where the time goes in v3:
time: 138 us
  Pallas kernels  134 us (97%)
  other arithmetic  3.16 us (2%)
    pallas_call x1, Pallas kernels, local_paired(): pl.pallas_call(functools.partial(iteration_kernel, period, normalizer, st...  134 us
    add x1, other arithmetic, local_paired(): estimate + (momentum_now - 1.0) / momentum_next * (estimate - previous)  3.16 us

profile of v3, /device:TPU:0, one launch (start us, length us, event | category | flops | bytes accessed | tf_op | source)
XLA Modules:
  0.0 138.2 jit_solution(17618228237944252918)
XLA Ops:
  1.4 133.6 %shard_map.104 = (f32[8,2,128,128]{3,2,1,0:T(8,128)}, f32[128,128]{1,0:T(8,128)}) custom-call(f32[2,16,64,2048]{3,2,1,0:T(8,128)} %spectra.1, f32[8,2,128,128]{3,2,1,0:T(8,128)} %current_in.1, s32[64,512]{1,0:T(8,128)} %table.1, s32[1,2048]{1,0:T(1,128)} %bitcast.6, f32[2,2048]{1,0:T(2,128)} %offsets.1, f32[2,512]{1,0:T(2,128)} %slowness.1, f32[1,128]{1,0:T(1,128)} %bitcast.7), custom_call_target="tpu_custom_call" | custom-call | flops 17179869184 | bytes 25165824 | tf_op jit(solution)/shard_map/pallas_call | solution.py:621
  135.0 3.2 %multiply_add_fusion = (f32[8,2,128,128]{3,2,1,0:T(8,128)}, f32[8,2,128,128]{3,2,1,0:T(8,128)}) fusion(f32[8,2,128,128]{3,2,1,0:T(8,128)} %param.11, f32[]{:T(128)S(6)} %div.7, f32[8,2,128,128]{3,2,1,0:T(8,128)} %get-tuple-element.4, f32[128,128]{1,0:T(8,128)} %get-tuple-element.5), kind=kLoop, calls=%fused_computation | loop fusion | flops 1048576 | bytes 4259844 | tf_op jit(solution)/shard_map/add | solution.py:668

commit v4 on v3

--- a/solution.py
+++ b/solution.py
@@ -347,7 +347,7 @@
                 start_chain(0, unit, turn, cs_a, t, (row, col, col_s))
             return 0
 
-        lax.fori_loop(0, cells // ROWS, strip, 0, unroll=4)
+        lax.fori_loop(0, cells // ROWS, strip, 0, unroll=8)
         send_unit(0, t)
 
         @pl.when(t >= 2)

time: 138 us -> 139 us (level)
  no operation moved by 1% of the time
where the time goes in v4:
time: 139 us; the launch traced here: 138 us
  Pallas kernels  134 us (96%)
  other arithmetic  3.16 us (2%)
    pallas_call x1, Pallas kernels, local_paired(): pl.pallas_call(functools.partial(iteration_kernel, period, normalizer, st...  134 us
    add x1, other arithmetic, local_paired(): estimate + (momentum_now - 1.0) / momentum_next * (estimate - previous)  3.16 us

profile of v4, /device:TPU:0, one launch (start us, length us, event | category | flops | bytes accessed | tf_op | source)
XLA Modules:
  0.0 138.3 jit_solution(2369989347922863153)
XLA Ops:
  1.4 133.8 %shard_map.104 = (f32[8,2,128,128]{3,2,1,0:T(8,128)}, f32[128,128]{1,0:T(8,128)}) custom-call(f32[2,16,64,2048]{3,2,1,0:T(8,128)} %spectra.1, f32[8,2,128,128]{3,2,1,0:T(8,128)} %current_in.1, s32[64,512]{1,0:T(8,128)} %table.1, s32[1,2048]{1,0:T(1,128)} %bitcast.6, f32[2,2048]{1,0:T(2,128)} %offsets.1, f32[2,512]{1,0:T(2,128)} %slowness.1, f32[1,128]{1,0:T(1,128)} %bitcast.7), custom_call_target="tpu_custom_call" | custom-call | flops 17179869184 | bytes 25165824 | tf_op jit(solution)/shard_map/pallas_call | solution.py:621
  135.2 3.2 %multiply_add_fusion = (f32[8,2,128,128]{3,2,1,0:T(8,128)}, f32[8,2,128,128]{3,2,1,0:T(8,128)}) fusion(f32[8,2,128,128]{3,2,1,0:T(8,128)} %param.11, f32[]{:T(128)S(6)} %div.7, f32[8,2,128,128]{3,2,1,0:T(8,128)} %get-tuple-element.4, f32[128,128]{1,0:T(8,128)} %get-tuple-element.5), kind=kLoop, calls=%fused_computation | loop fusion | flops 1048576 | bytes 4259844 | tf_op jit(solution)/shard_map/add | solution.py:668
